TPU v7x, 32 devices: a whole 2x2x4 slice. The times are simulated.
32 devices in a mesh: gx: 2 (over y), gy: 2 (over x), vert: 8 (over z, core).
Axes of the slice: x: 2, y: 2, z: 4, core: 2. Of those that a mesh axis runs over, the one named last changes fastest.
Arguments:
- state: float32 [8000, 3, 4, 256], P('vert', None, 'gy', 'gx'), as said below
- tangent: float32 [8000, 3, 4, 256], P('vert', None, 'gy', 'gx')
- orient: int32 [8000, 2], P('vert'), may hold values from 0 to 1, as said below
- walls: int32 [2, 256], P(None, 'gx'), may hold values from 0 to 1
Outputs:
- product: float32 [8000, 3, 4, 256], P('vert', None, 'gy', 'gx')
Inputs may be any that keep to these rules, and one draw needn't show every extreme that they name: In every aligned group of four slots 4k to 4k+3 there are two bits p, r with orient[4k + 2b + e] = (e XOR p, b XOR r) for b, e in 0, 1. The state's values at the four points q of every cell are positive.
All inputs are finite; a program needn't handle non-finite values.
Results may differ from a plain program's by a relative error of at most 0.0003.
Values sent between devices are 32-bit elements; how exact they have to be, the bound alone decides.
No kernel may reach another device: no remote copies, remote signals or barrier semaphores. Data moves between devices by JAX's collectives and lax.ppermute only.
A program may use at most 64 MiB of HBM per device.

v0:
```python
import math

import jax
import jax.numpy as jnp
from jax import lax
from jax.sharding import PartitionSpec as P

NVX = 20


GAUSS = 0.5773502691896258
XI_SIGNS = (-1.0, -1.0, 1.0, 1.0)
ETA_SIGNS = (-1.0, 1.0, -1.0, 1.0)
MIRRORED_DUOS = ((0, 0), (1, 1), (2, 2), (0, 1), (0, 2), (1, 2))
COLLIDE = 2.0
LOG_TWO_PI = math.log(2.0 * math.pi)


def from_behind(array, axis, by):
    devices = lax.axis_size(axis)
    return lax.ppermute(array, axis, [(i, (i + by) % devices) for i in range(devices)])


def from_behind_2(value, axis, steps):
    count = lax.axis_size(axis)
    initial, last = (max(0, -steps), min(count, count - steps))
    return lax.ppermute(value, axis, [(source, source + steps) for source in range(initial, last)])


def velocities(slot_index, orient, half_grid):
    spacing = 5.0 / half_grid
    mag_x = (slot_index // (4 * half_grid) % half_grid).astype(jnp.float32) + 0.5
    mag_y = (slot_index // 4 % half_grid).astype(jnp.float32) + 0.5
    level_z = (slot_index // (4 * half_grid * half_grid)).astype(jnp.float32) - (half_grid - 0.5)
    sign_x = (2 * orient[:, 0] - 1).astype(jnp.float32)
    sign_y = (2 * orient[:, 1] - 1).astype(jnp.float32)
    return (sign_x * mag_x * spacing, sign_y * mag_y * spacing, level_z * spacing)


def moment_table(vel_x, vel_y, molecular_grid_extent, weight):
    return (
        jnp.stack(
            [
                jnp.ones_like(vel_x),
                vel_x,
                vel_y,
                molecular_grid_extent,
                vel_x * vel_x,
                vel_y * vel_y,
                molecular_grid_extent * molecular_grid_extent,
                vel_x * vel_y,
                vel_x * molecular_grid_extent,
                vel_y * molecular_grid_extent,
            ]
        )
        * weight
    )


def gauss_points(coef):
    center, grad_x, grad_y = (coef[:, 0], coef[:, 1], coef[:, 2])
    return jnp.stack(
        [center + XI_SIGNS[q] * GAUSS * grad_x + ETA_SIGNS[q] * GAUSS * grad_y for q in range(4)],
        axis=1,
    )


def project_points(values):
    total = values[:, 0] + values[:, 1] + values[:, 2] + values[:, 3]
    along_x = values[:, 2] + values[:, 3] - (values[:, 0] + values[:, 1])
    along_y = values[:, 1] + values[:, 3] - (values[:, 0] + values[:, 2])
    return jnp.stack([0.25 * total, 0.75 * GAUSS * along_x, 0.75 * GAUSS * along_y], axis=1)


def partner(values):
    dims_in = values.shape
    grouped = values.reshape((dims_in[0] // 4, 2, 2) + dims_in[1:])
    return grouped[:, ::-1].reshape(dims_in)


def full_matrix(entries):
    rows = [[None, None, None], [None, None, None], [None, None, None]]
    for duo_ordinal, (leading_multiplier, trailing_multiplier) in enumerate(MIRRORED_DUOS):
        rows[leading_multiplier][trailing_multiplier] = entries[duo_ordinal]
        rows[trailing_multiplier][leading_multiplier] = entries[duo_ordinal]
    return rows


def gauss_params(moments):
    density = moments[0]
    average_offset = [moments[1 + leading_multiplier] / density for leading_multiplier in range(3)]
    second = [moments[4 + duo_ordinal] for duo_ordinal in range(6)]
    covariance_array = [
        second[duo_ordinal] / density
        - average_offset[leading_multiplier] * average_offset[trailing_multiplier]
        for duo_ordinal, (leading_multiplier, trailing_multiplier) in enumerate(MIRRORED_DUOS)
    ]
    thermal_state = (covariance_array[0] + covariance_array[1] + covariance_array[2]) / 3.0
    pressure_dyad = [
        (1.5 * thermal_state if leading_multiplier == trailing_multiplier else 0.0)
        - 0.5 * covariance_array[duo_ordinal]
        for duo_ordinal, (leading_multiplier, trailing_multiplier) in enumerate(MIRRORED_DUOS)
    ]
    tens_full = full_matrix(pressure_dyad)
    cofactor = [
        tens_full[1][1] * tens_full[2][2] - tens_full[1][2] * tens_full[1][2],
        tens_full[0][0] * tens_full[2][2] - tens_full[0][2] * tens_full[0][2],
        tens_full[0][0] * tens_full[1][1] - tens_full[0][1] * tens_full[0][1],
        tens_full[0][2] * tens_full[1][2] - tens_full[0][1] * tens_full[2][2],
        tens_full[0][1] * tens_full[1][2] - tens_full[0][2] * tens_full[1][1],
        tens_full[0][1] * tens_full[0][2] - tens_full[0][0] * tens_full[1][2],
    ]
    determinant = (
        tens_full[0][0] * cofactor[0]
        + tens_full[0][1] * cofactor[3]
        + tens_full[0][2] * cofactor[4]
    )
    inverse = [entry / determinant for entry in cofactor]
    log_pre = jnp.log(density) - 1.5 * LOG_TWO_PI - 0.5 * jnp.log(determinant)
    delta_density = moments[10]
    drift_delta = [
        (moments[11 + leading_multiplier] - average_offset[leading_multiplier] * delta_density)
        / density
        for leading_multiplier in range(3)
    ]
    dtheta = [
        moments[14 + duo_ordinal] / density
        - second[duo_ordinal] * delta_density / (density * density)
        - (
            drift_delta[leading_multiplier] * average_offset[trailing_multiplier]
            + average_offset[leading_multiplier] * drift_delta[trailing_multiplier]
        )
        for duo_ordinal, (leading_multiplier, trailing_multiplier) in enumerate(MIRRORED_DUOS)
    ]
    temp_delta = (dtheta[0] + dtheta[1] + dtheta[2]) / 3.0
    tens_delta = [
        (1.5 * temp_delta if leading_multiplier == trailing_multiplier else 0.0)
        - 0.5 * dtheta[duo_ordinal]
        for duo_ordinal, (leading_multiplier, trailing_multiplier) in enumerate(MIRRORED_DUOS)
    ]
    inv_full = full_matrix(inverse)
    delta_full = full_matrix(tens_delta)
    trace_term = sum(
        [
            inv_full[leading_multiplier][trailing_multiplier]
            * delta_full[trailing_multiplier][leading_multiplier]
            for leading_multiplier in range(3)
            for trailing_multiplier in range(3)
        ]
    )
    shift_term = delta_density / density - 0.5 * trace_term
    weight_vec = [
        inv_full[leading_multiplier][0] * drift_delta[0]
        + inv_full[leading_multiplier][1] * drift_delta[1]
        + inv_full[leading_multiplier][2] * drift_delta[2]
        for leading_multiplier in range(3)
    ]
    inner_prod = [
        [
            inv_full[leading_multiplier][0] * delta_full[0][c]
            + inv_full[leading_multiplier][1] * delta_full[1][c]
            + inv_full[leading_multiplier][2] * delta_full[2][c]
            for c in range(3)
        ]
        for leading_multiplier in range(3)
    ]
    curve_sym = [
        inner_prod[leading_multiplier][0] * inv_full[0][trailing_multiplier]
        + inner_prod[leading_multiplier][1] * inv_full[1][trailing_multiplier]
        + inner_prod[leading_multiplier][2] * inv_full[2][trailing_multiplier]
        for leading_multiplier, trailing_multiplier in MIRRORED_DUOS
    ]
    return jnp.stack(average_offset + inverse + [log_pre, shift_term] + weight_vec + curve_sym)


def quadratic(entries, rel_x, rel_y, rel_z):
    return (
        entries[0] * rel_x * rel_x
        + entries[1] * rel_y * rel_y
        + entries[2] * rel_z * rel_z
        + 2.0
        * (entries[3] * rel_x * rel_y + entries[4] * rel_x * rel_z + entries[5] * rel_y * rel_z)
    )


def gauss_tangent(vel_x, vel_y, molecular_grid_extent, params):
    rel_x = vel_x[:, None] - params[0]
    rel_y = vel_y[:, None] - params[1]
    rel_z = molecular_grid_extent[:, None] - params[2]
    gauss = jnp.exp(params[9] - 0.5 * quadratic(params[3:9], rel_x, rel_y, rel_z))
    return gauss * (
        params[10]
        + rel_x * params[11]
        + rel_y * params[12]
        + rel_z * params[13]
        + 0.5 * quadratic(params[14:20], rel_x, rel_y, rel_z)
    )


def transport(coef, orient, vel_x, vel_y, left_in, right_in, below_in, above_in):
    center, grad_x, grad_y = (coef[:, 0], coef[:, 1], coef[:, 2])
    heads_right = (orient[:, 0] == 1)[:, None, None]
    heads_up = (orient[:, 1] == 1)[:, None, None]
    right_val = jnp.where(heads_right, center + grad_x, right_in[0])
    right_slope = jnp.where(heads_right, grad_y, right_in[1])
    left_val = jnp.where(heads_right, left_in[0], center - grad_x)
    left_slope = jnp.where(heads_right, left_in[1], grad_y)
    top_val = jnp.where(heads_up, center + grad_y, above_in[0])
    top_slope = jnp.where(heads_up, grad_x, above_in[1])
    bottom_val = jnp.where(heads_up, below_in[0], center - grad_y)
    bottom_slope = jnp.where(heads_up, below_in[1], grad_x)
    speed_x = vel_x[:, None, None]
    speed_y = vel_y[:, None, None]
    rate_mean = speed_x * (right_val - left_val) + speed_y * (top_val - bottom_val)
    rate_x = 3.0 * speed_x * (right_val + left_val - 2.0 * center) + speed_y * (
        top_slope - bottom_slope
    )
    rate_y = speed_x * (right_slope - left_slope) + 3.0 * speed_y * (
        top_val + bottom_val - 2.0 * center
    )
    return jnp.stack([rate_mean, rate_x, rate_y], axis=1)


def pick_pair(values, selector, stride):
    dims_in = values.shape
    grouped = values.reshape((dims_in[0] // (2 * stride), 2, stride) + dims_in[1:])
    chosen = selector.reshape(dims_in[0] // (2 * stride), 2, stride)[:, 0] == 1
    chosen = chosen.reshape(chosen.shape + (1,) * (len(dims_in) - 1))
    return jnp.where(chosen, grouped[:, 0], grouped[:, 1])


def spread_pair(pieces, selector):
    slots_here = selector.shape[0]
    widened = jnp.broadcast_to(pieces[:, None], (pieces.shape[0], 2) + pieces.shape[1:])
    widened = widened.reshape((slots_here,) + pieces.shape[2:])
    mask_rows = (selector == 1).reshape((slots_here,) + (1,) * (len(pieces.shape) - 2))
    return jnp.where(mask_rows, widened, 0.0)


def shards(state, tangent, orient, walls):
    slots_here = state.shape[0]
    cell_rows = state.shape[2]
    cell_cols = state.shape[3]
    half_grid = NVX // 2
    weight = (5.0 / half_grid) ** 3
    point_count = 4 * cell_rows * cell_cols
    slot_index = lax.axis_index("vert") * slots_here + jnp.arange(slots_here, dtype=jnp.int32)
    vel_x, vel_y, molecular_grid_extent = velocities(slot_index, orient, half_grid)
    moment_rows = moment_table(vel_x, vel_y, molecular_grid_extent, weight)
    stacked = jnp.concatenate(
        [
            gauss_points(state).reshape(slots_here, point_count),
            gauss_points(tangent).reshape(slots_here, point_count),
        ],
        axis=1,
    )
    partial_sums = jnp.dot(
        moment_rows, stacked, precision=lax.Precision.HIGHEST, preferred_element_type=jnp.float32
    )
    partial_sums = jnp.concatenate(
        [partial_sums[:, :point_count], partial_sums[:, point_count:]], axis=0
    )
    params = gauss_params(lax.psum(partial_sums, "vert"))
    center, grad_x, grad_y = (tangent[:, 0], tangent[:, 1], tangent[:, 2])
    heads_right = orient[:, 0]
    heads_up = orient[:, 1]
    right_face = jnp.stack([center[:, :, -1] + grad_x[:, :, -1], grad_y[:, :, -1]], axis=1)
    received = from_behind(pick_pair(right_face, heads_right, 1), "gx", 1)
    edge_rows = spread_pair(received, heads_right)
    left_in = (
        jnp.concatenate([edge_rows[:, 0, :, None], (center + grad_x)[:, :, :-1]], axis=2),
        jnp.concatenate([edge_rows[:, 1, :, None], grad_y[:, :, :-1]], axis=2),
    )
    left_face = jnp.stack([center[:, :, 0] - grad_x[:, :, 0], grad_y[:, :, 0]], axis=1)
    received = from_behind(pick_pair(left_face, 1 - heads_right, 1), "gx", -1)
    edge_rows = spread_pair(received, 1 - heads_right)
    right_in = (
        jnp.concatenate([(center - grad_x)[:, :, 1:], edge_rows[:, 0, :, None]], axis=2),
        jnp.concatenate([grad_y[:, :, 1:], edge_rows[:, 1, :, None]], axis=2),
    )
    top_face = jnp.stack([center[:, -1] + grad_y[:, -1], grad_x[:, -1]], axis=1)
    received = from_behind_2(pick_pair(top_face, heads_up, 2), "gy", 1)
    edge_rows = spread_pair(received, heads_up)
    below_in = (
        jnp.concatenate([edge_rows[:, 0:1], (center + grad_y)[:, :-1]], axis=1),
        jnp.concatenate([edge_rows[:, 1:2], grad_x[:, :-1]], axis=1),
    )
    bottom_face = jnp.stack([center[:, 0] - grad_y[:, 0], grad_x[:, 0]], axis=1)
    received = from_behind_2(pick_pair(bottom_face, 1 - heads_up, 2), "gy", -1)
    edge_rows = spread_pair(received, 1 - heads_up)
    above_in = (
        jnp.concatenate([(center - grad_y)[:, 1:], edge_rows[:, 0:1]], axis=1),
        jnp.concatenate([grad_x[:, 1:], edge_rows[:, 1:2]], axis=1),
    )
    floor_flag = walls[0].astype(jnp.float32)
    roof_flag = walls[1].astype(jnp.float32)
    at_bottom = lax.axis_index("gy") == 0
    at_top = lax.axis_index("gy") == lax.axis_size("gy") - 1
    floor_val = (floor_flag * partner(center - grad_y)[:, 0], floor_flag * partner(grad_x)[:, 0])
    roof_val = (roof_flag * partner(center + grad_y)[:, -1], roof_flag * partner(grad_x)[:, -1])
    below_in = tuple(
        (
            jnp.concatenate(
                [jnp.where(at_bottom, wall_part, field_part[:, 0])[:, None], field_part[:, 1:]],
                axis=1,
            )
            for field_part, wall_part in zip(below_in, floor_val)
        )
    )
    above_in = tuple(
        (
            jnp.concatenate(
                [field_part[:, :-1], jnp.where(at_top, wall_part, field_part[:, -1])[:, None]],
                axis=1,
            )
            for field_part, wall_part in zip(above_in, roof_val)
        )
    )
    advected = transport(tangent, orient, vel_x, vel_y, left_in, right_in, below_in, above_in)
    gauss_delta = gauss_tangent(vel_x, vel_y, molecular_grid_extent, params).reshape(
        slots_here, 4, cell_rows, cell_cols
    )
    return advected + COLLIDE * (tangent - project_points(gauss_delta))


def solution(mesh):
    placed = (
        P("vert", None, "gy", "gx"),
        P("vert", None, "gy", "gx"),
        P("vert", None),
        P(None, "gx"),
    )
    return jax.shard_map(
        shards, mesh=mesh, in_specs=placed, out_specs=P("vert", None, "gy", "gx"), check_vma=False
    )
```

profile of v0, /device:TPU:0, one launch (start us, length us, event | category | flops | bytes accessed | tf_op | source)
XLA Modules:
  0.0 135.7 jit_solution(15435599997230172240)
XLA Ops:
  6.5 0.9 fusion.101
  7.6 2.1 %copy.136 = f32[1000,3,2,128]{3,0,2,1:T(8,128)S(1)} copy(f32[1000,3,2,128]{3,2,1,0:T(2,128)} %param.5) | data formatting | bytes 6144000 | tf_op args[1]
  9.7 2.5 %multiply_add_fusion.8 = (f32[1000,1,2,128]{3,0,2,1:T(8,128)S(1)}, f32[1000,2,128]{2,0,1:T(8,128)}, f32[1000,1,2,128]{3,0,2,1:T(8,128)}, f32[1000,1,2,128]{3,0,2...) fusion(f32[1000,3,2,128]{3,0,2,1:T(8,128)S(1)} %copy.136), kind=kLoop, calls=%fused_computation.101 | loop fusion | flops 3072000 | bytes 12288000 | tf_op jit(solution)/shard_map/add | solution.py:63
  12.1 2.3 %pad_maximum_fusion.1 = f32[1000,4,2,128]{3,0,2,1:T(8,128)} fusion(f32[1000,1,2,128]{3,0,2,1:T(8,128)S(1)} %get-tuple-element.79, f32[1000,1,2,128]{3,0,2,1:T(8,128)S(1)} %get-tuple-element.80, f32[1000,1,2,128]{3,0,2,1:T(8,128)S(1)} %get-tuple-element.78, f32[1000,1,2,128]{3,0,2,1:T(8,128)S(1)} %get-tuple-element.74), kind=kLoop, calls=%fused_computation.53 | loop fusion | flops 3072000 | bytes 8192000 | tf_op jit(solution)/shard_map/stack | solution.py:62
  14.4 5.3 %copy.157 = f32[1000,4,2,128]{0,3,2,1:T(8,128)} copy(f32[1000,4,2,128]{3,0,2,1:T(8,128)} %pad_maximum_fusion.1) | data formatting | bytes 8192000 | tf_op jit(solution)/shard_map/stack | solution.py:62
  19.7 2.0 %fusion.121 = (f32[1000,1,2,128]{3,2,1,0:T(2,128)S(1)}, f32[1000,1,2,128]{3,2,1,0:T(2,128)S(1)}, f32[1000,1,2,128]{3,2,1,0:T(2,128)S(1)}) fusion(f32[1000,3,2,128]{3,2,1,0:T(2,128)} %param.4), kind=kLoop, calls=%fused_computation.320 | loop fusion | bytes 6144000 | tf_op jit(solution)/shard_map/slice | solution.py:61
  21.8 0.4 fusion.37
  22.2 2.2 %pad_maximum_fusion = f32[1000,4,2,128]{3,0,2,1:T(8,128)} fusion(f32[1000,1,2,128]{3,0,2,1:T(8,128)S(1)} %get-tuple-element.68, f32[1000,1,2,128]{3,0,2,1:T(8,128)S(1)} %get-tuple-element.69, f32[1000,1,2,128]{3,0,2,1:T(8,128)S(1)} %get-tuple-element.70, f32[1000,1,2,128]{3,0,2,1:T(8,128)S(1)} %get-tuple-element.67), kind=kLoop, calls=%fused_computation.52 | loop fusion | flops 3072000 | bytes 8192000 | tf_op jit(solution)/shard_map/stack | solution.py:62
  24.4 5.3 %copy.156 = f32[1000,4,2,128]{0,3,2,1:T(8,128)} copy(f32[1000,4,2,128]{3,0,2,1:T(8,128)} %pad_maximum_fusion) | data formatting | bytes 8192000 | tf_op jit(solution)/shard_map/stack | solution.py:62
  29.8 9.2 %fusion = f32[10,2048]{1,0:T(8,128)S(1)} fusion(f32[1000,1024]{0,1:T(8,128)} %bitcast.144, f32[1000,1024]{0,1:T(8,128)} %bitcast.145, f32[10,1000]{1,0:T(8,128)S(1)} %stack.41), kind=kOutput, calls=%fused_computation.27 | convolution fusion | flops 247818000 | bytes 8313920 | tf_op jit(solution)/shard_map/dot_general | solution.py:257
  39.0 0.7 pad_maximum_fusion.4
  39.8 1.0 copy-done
  40.8 1.4 %slice_bitcast_fusion.9 = (f32[1000,1,1,128]{3,0,2,1:T(8,128)}, f32[1000,1,1,128]{3,0,2,1:T(8,128)}, f32[1000,1,128]{2,0,1:T(8,128)}, f32[1000,1,128]{2,0,1:T(8,128)}) fusion(f32[1000,2,128]{2,0,1:T(8,128)S(1)} %slice_bitcast_fusion.10), kind=kLoop, calls=%fused_computation.318 | loop fusion | bytes 3072000 | tf_op jit(solution)/shard_map/concatenate | solution.py:303
  42.3 0.4 squeeze.34
  43.1 2.8 %subtract_bitcast_fusion = (f32[1000,1,1,128]{3,0,2,1:T(8,128)}, f32[1000,1,1,128]{3,0,2,1:T(8,128)}, f32[1000,1,128]{2,0,1:T(8,128)S(1)}, f32[1000,1,128]{2,0,1:T(8,128)}) fusion(f32[1000,2,128]{2,0,1:T(8,128)} %get-tuple-element.81, f32[1000,2,128]{2,0,1:T(8,128)} %get-tuple-element.75), kind=kLoop, calls=%fused_computation.135 | loop fusion | flops 512000 | bytes 4096000 | tf_op jit(solution)/shard_map/concatenate | solution.py:312
  45.9 1.6 %fusion.45 = f32[250,2,2,128]{3,1,0,2:T(2,128)} fusion(f32[250,2,2,1,128]{4,2,1,0,3:T(2,128)S(1)} %bitcast.155, f32[250,2,2,1,128]{4,2,1,0,3:T(2,128)S(1)} %bitcast.157, pred[250,2]{1,0:T(8,128)(4,1)S(1)} %copy.146), kind=kLoop, calls=%fused_computation.115 | loop fusion | flops 384000 | bytes 1536500 | tf_op jit(solution)/shard_map/jit(_where)/select_n | solution.py:229
  47.5 1.3 collective-permute-start.2
  48.9 2.7 %fusion.42 = f32[250,2,2,128]{3,1,0,2:T(2,128)} fusion(f32[250,2,2,1,128]{4,2,1,0,3:T(2,128)} %bitcast.154, f32[250,2,2,1,128]{4,2,1,0,3:T(2,128)} %bitcast.156, pred[250,2]{1,0:T(8,128)(4,1)S(1)} %copy.149), kind=kLoop, calls=%fused_computation.112 | loop fusion | flops 384000 | bytes 1536500 | tf_op jit(solution)/shard_map/jit(_where)/select_n | solution.py:229
  51.6 6.4 %collective-permute-start.3 = (f32[250,2,2,128]{3,1,0,2:T(2,128)}, f32[250,2,2,128]{3,1,0,2:T(2,128)}, u32[]{:S(2)}, u32[]{:S(2)}) collective-permute-start(f32[250,2,2,128]{3,1,0,2:T(2,128)} %fusion.42), channel_id=1, source_target_pairs={{0,8},{1,9},{2,10},{3,11},{4,12},{5,13},{6,14},{7,15},{16,24},{17,... | collective-permute-start | bytes 1536008 | tf_op jit(solution)/shard_map/ppermute | solution.py:27
  58.0 5.0 %slice_reduce_fusion = (f32[1000,2]{0,1:T(2,128)S(1)}, f32[1000,2]{0,1:T(2,128)S(1)}, f32[1000,2]{0,1:T(2,128)S(1)}, f32[1000,2]{0,1:T(2,128)S(1)}) fusion(f32[1000,2,128]{2,0,1:T(8,128)} %get-tuple-element.81, f32[1000,2,128]{2,0,1:T(8,128)} %copy-done, f32[1000,2,128]{2,0,1:T(8,128)} %get-tuple-element.75), kind=kLoop, calls=%fused_computation.61 | loop fusion | flops 4000 | bytes 80000 | tf_op jit(solution)/shard_map/slice | solution.py:267
  63.0 1.1 add.987
  64.1 1.2 copy.142
  65.3 1.1 stack.32
  66.4 1.2 copy.143
  68.1 2.7 %collective-permute-start.1 = (f32[500,1,2,2]{0,3,2,1:T(2,128)S(1)}, f32[500,1,2,2]{0,3,2,1:T(2,128)S(1)}, u32[]{:S(2)}, u32[]{:S(2)}) collective-permute-start(f32[500,1,2,2]{0,3,2,1:T(2,128)S(1)} %fusion.57), channel_id=1, source_target_pairs={{0,16},{16,0},{1,17},{17,1},{2,18},{18,2},{3,19},{19,3},{4,20},{20... | collective-permute-start | bytes 24008 | tf_op jit(solution)/shard_map/ppermute | solution.py:21
  70.8 1.1 sub.770
  71.9 1.2 copy.139
  73.1 1.1 stack.30
  74.2 1.2 copy.140
  75.5 5.8 %slice_bitcast_fusion = (f32[1000,1,2,127]{3,0,2,1:T(8,128)}, f32[1000,1,2,127]{3,0,2,1:T(8,128)}, f32[1000,1,2,127]{3,0,2,1:T(8,128)}, f32[1000,1,2,127]{3,0,2,1:T(8,128)}) fusion(f32[1000,2,128]{2,0,1:T(8,128)} %get-tuple-element.81, f32[1000,2,128]{2,0,1:T(8,128)} %copy-done, f32[1000,2,128]{2,0,1:T(8,128)} %get-tuple-element.75), kind=kLoop, calls=%fused_computation.57 | loop fusion | flops 508000 | bytes 10160000 | tf_op jit(solution)/shard_map/concatenate | solution.py:272
  81.4 2.6 %rev.10 = f32[250,2,2,2,128]{4,2,1,0,3:T(2,128)} reverse(f32[250,2,2,2,128]{4,2,1,0,3:T(2,128)} %bitcast.146), dimensions={1} | reverse | bytes 2048000 | tf_op jit(solution)/shard_map/rev | solution.py:78
  84.0 2.6 %rev.11 = f32[250,2,2,2,128]{4,2,1,0,3:T(2,128)} reverse(f32[250,2,2,2,128]{4,2,1,0,3:T(2,128)} %bitcast.147), dimensions={1} | reverse | bytes 2048000 | tf_op jit(solution)/shard_map/rev | solution.py:78
  86.6 2.5 %rev.12 = f32[250,2,2,2,128]{4,2,1,0,3:T(2,128)} reverse(f32[250,2,2,2,128]{4,2,1,0,3:T(2,128)} %bitcast.150), dimensions={1} | reverse | bytes 2048000 | tf_op jit(solution)/shard_map/rev | solution.py:78
  89.2 1.3 broadcast_in_dim.150
  90.5 1.7 %broadcast_in_dim.151 = f32[1000,2,2]{0,2,1:T(2,128)S(1)} reshape(f32[500,2,2,2]{1,0,3,2:T(8,128)} %broadcast_in_dim.150) | data formatting | bytes 32000 | tf_op jit(solution)/shard_map/broadcast_in_dim | solution.py:234
  92.2 1.3 broadcast_in_dim.144
  93.5 1.7 %broadcast_in_dim.145 = f32[1000,2,2]{0,2,1:T(2,128)S(1)} reshape(f32[500,2,2,2]{1,0,3,2:T(8,128)} %broadcast_in_dim.144) | data formatting | bytes 32000 | tf_op jit(solution)/shard_map/broadcast_in_dim | solution.py:234
  95.2 1.4 %copy.144 = f32[1000,1,2,1]{3,0,2,1:T(8,128)} copy(f32[1000,1,2,1]{0,2,3,1:T(2,128)S(1)} %get-tuple-element.125) | data formatting | bytes 16000 | tf_op jit(solution)/shard_map/concatenate | solution.py:271
  96.6 1.3 copy.141
  98.0 1.4 %copy.152 = f32[1000,1,2,1]{3,0,2,1:T(8,128)} copy(f32[1000,1,2,1]{0,2,3,1:T(2,128)S(1)} %get-tuple-element.126) | data formatting | bytes 16000 | tf_op jit(solution)/shard_map/concatenate | solution.py:272
  99.3 1.3 copy.151
  100.7 1.1 multiply_subtract_fusion.2
  101.8 1.0 multiply_subtract_fusion.1
  102.8 1.0 multiply_subtract_fusion.10
  103.8 1.1 multiply_subtract_fusion.3
  105.1 8.0 %fusion.10 = f32[1000,4,2,128]{3,0,2,1:T(8,128)S(1)} fusion(f32[4,2,128]{2,1,0:T(2,128)S(1)} %bitcast.177, f32[4,2,128]{2,1,0:T(2,128)S(1)} %bitcast.180, f32[4,2,128]{2,1,0:T(2,128)S(1)} %bitcast.179, f32[4,2,128]{2,1,0:T(2,128)S(1)} %bitcast.178, f32[4,2,128]{2,1,0:T(2,128)S(1)} %bitcast.181, f32[4,2,128]{2,1,0:T(2,128)S(1)} %bitcast.176, ...), kind=kLoop, calls=%fused_computation.37 | loop fusion | flops 51200000 | bytes 4189920 | tf_op jit(solution)/shard_map/mul | solution.py:191
  113.0 0.4 add_multiply_fusion
  113.5 1.5 %broadcast_in_dim.155 = f32[250,2,2,2,128]{4,2,1,0,3:T(2,128)S(1)} broadcast(f32[250,2,2,128]{3,1,0,2:T(2,128)} %collective-permute-done.2), dimensions={0,2,3,4} | broadcast | bytes 1536000 | tf_op jit(solution)/shard_map/broadcast_in_dim | solution.py:234
  114.9 1.3 broadcast_in_dim.159
  116.3 0.3 broadcast_select_fusion
  116.9 0.5 copy-done.13
  117.5 0.4 copy-done.1
  117.9 0.3 copy-done.2
  118.5 0.3 copy-done.8
  118.8 0.3 copy-done.9
  119.1 0.3 copy-done.12
  119.4 1.5 %multiply_add_fusion.4 = (f32[1000,1,2,128]{3,0,2,1:T(8,128)S(1)}, f32[1000,1,2,128]{3,0,2,1:T(8,128)S(1)}, f32[1000,1,2,128]{3,0,2,1:T(8,128)S(1)}) fusion(f32[1000]{0:T(1024)S(1)} %get-tuple-element.134, f32[1000]{0:T(1024)S(1)} %get-tuple-element.133, f32[1000,1,2,128]{3,0,2,1:T(8,128)S(1)} %copy-done.2, f32[1000,1,1,128]{3,0,2,1:T(8,128)S(1)} %copy-done.5, ...), kind=kLoop, calls=%fused_computation.94 | loop fusion | flops 3840000 | bytes 11274000 | tf_op jit(solution)/shard_map/add | solution.py:214
  120.9 0.3 copy-done.10
  121.2 0.3 copy-done.11
  121.6 1.4 %fusion.35 = f32[1000,1,2,128]{3,0,2,1:T(8,128)S(1)} fusion(f32[1000,1,2,1]{3,0,2,1:T(8,128)S(1)} %copy-done.11, f32[1000,1,2,127]{3,0,2,1:T(8,128)S(1)} %copy-done.7, f32[1000,1,2,127]{3,0,2,1:T(8,128)S(1)} %copy-done.6, f32[1000,1,2,1]{3,0,2,1:T(8,128)S(1)} %copy-done.10, f32[1000,3,2,128]{3,0,2,1:T(8,128)S(1)} %copy.136, f32[1000]{0:T(1024)S(1)} %get-tuple-element.135, ...), kind=kLoop, calls=%fused_computation.85 | loop fusion | flops 3840000 | bytes 9226000 | tf_op jit(solution)/shard_map/add | solution.py:218
  123.0 1.0 fusion.32
  124.0 0.8 copy-done.3
  124.9 0.7 maximum_add_fusion
  125.6 3.2 %copy.159 = f32[1000,3,2,128]{3,2,1,0:T(2,128)} copy(f32[1000,3,2,128]{3,0,2,1:T(8,128)S(1)} %maximum_add_fusion) | data formatting | bytes 6144000 | tf_op jit(solution)/shard_map/add | solution.py:323
  (71 shorter events, 2.3 us)
Async XLA Ops:
  6.5 94.1 %all-reduce.2.cloned.1.call-start = ((), (), s32[]{:S(2)}) async-start(), calls=%async_computation | async-start | bytes 196608 | tf_op jit(solution)/shard_map/psum | solution.py:263
  29.8 10.0 %copy-start.20 = (s32[1000,2]{0,1:T(2,128)S(1)}, s32[1000,2]{0,1:T(2,128)}, u32[]{:S(2)}) copy-start(s32[1000,2]{0,1:T(2,128)} %param.6) | copy-start | bytes 24004
  39.8 1.1 copy-start
  43.1 2.8 %copy-start.17 = (f32[1000,1,128]{2,0,1:T(8,128)S(1)}, f32[1000,1,128]{2,0,1:T(8,128)}, u32[]{:S(2)}) copy-start(f32[1000,1,128]{2,0,1:T(8,128)} %get-tuple-element.98) | copy-start | bytes 1536004
  47.5 66.0 %collective-permute-start.2 = (f32[250,2,2,128]{3,1,0,2:T(2,128)}, f32[250,2,2,128]{3,1,0,2:T(2,128)}, u32[]{:S(2)}, u32[]{:S(2)}) collective-permute-start(f32[250,2,2,128]{3,1,0,2:T(2,128)} %fusion.45), channel_id=1, source_target_pairs={{8,0},{9,1},{10,2},{11,3},{12,4},{13,5},{14,6},{15,7},{24,16},{25,... | collective-permute-start | bytes 1536008 | tf_op jit(solution)/shard_map/ppermute | solution.py:27
  51.6 61.9 %collective-permute-start.3 = (f32[250,2,2,128]{3,1,0,2:T(2,128)}, f32[250,2,2,128]{3,1,0,2:T(2,128)}, u32[]{:S(2)}, u32[]{:S(2)}) collective-permute-start(f32[250,2,2,128]{3,1,0,2:T(2,128)} %fusion.42), channel_id=1, source_target_pairs={{0,8},{1,9},{2,10},{3,11},{4,12},{5,13},{6,14},{7,15},{16,24},{17,... | collective-permute-start | bytes 1536008 | tf_op jit(solution)/shard_map/ppermute | solution.py:27
  68.1 21.1 %collective-permute-start.1 = (f32[500,1,2,2]{0,3,2,1:T(2,128)S(1)}, f32[500,1,2,2]{0,3,2,1:T(2,128)S(1)}, u32[]{:S(2)}, u32[]{:S(2)}) collective-permute-start(f32[500,1,2,2]{0,3,2,1:T(2,128)S(1)} %fusion.57), channel_id=1, source_target_pairs={{0,16},{16,0},{1,17},{17,1},{2,18},{18,2},{3,19},{19,3},{4,20},{20... | collective-permute-start | bytes 24008 | tf_op jit(solution)/shard_map/ppermute | solution.py:21
  75.4 5.9 %copy-start.21 = (s32[2,128]{1,0:T(2,128)S(1)}, s32[2,128]{1,0:T(2,128)}, u32[]{:S(2)}) copy-start(s32[2,128]{1,0:T(2,128)} %param.7) | copy-start | bytes 3076
  75.5 16.8 %collective-permute-start = (f32[500,1,2,2]{0,3,2,1:T(2,128)S(1)}, f32[500,1,2,2]{0,3,2,1:T(2,128)S(1)}, u32[]{:S(2)}, u32[]{:S(2)}) collective-permute-start(f32[500,1,2,2]{0,3,2,1:T(2,128)S(1)} %fusion.60), channel_id=1, source_target_pairs={{0,16},{16,0},{1,17},{17,1},{2,18},{18,2},{3,19},{19,3},{4,20},{20... | collective-permute-start | bytes 24008 | tf_op jit(solution)/shard_map/ppermute | solution.py:21
  113.4 3.2 %copy-start.14 = (f32[250,2,2,2,128]{4,2,1,0,3:T(2,128)S(1)}, f32[250,2,2,2,128]{4,2,1,0,3:T(2,128)}, u32[]{:S(2)}) copy-start(f32[250,2,2,2,128]{4,2,1,0,3:T(2,128)} %rev.12) | copy-start | bytes 3072004
  113.4 3.2 %copy-start.15 = (f32[250,2,2,2,128]{4,2,1,0,3:T(2,128)S(1)}, f32[250,2,2,2,128]{4,2,1,0,3:T(2,128)}, u32[]{:S(2)}) copy-start(f32[250,2,2,2,128]{4,2,1,0,3:T(2,128)} %rev.10) | copy-start | bytes 3072004
  113.4 3.2 %copy-start.16 = (f32[250,2,2,2,128]{4,2,1,0,3:T(2,128)S(1)}, f32[250,2,2,2,128]{4,2,1,0,3:T(2,128)}, u32[]{:S(2)}) copy-start(f32[250,2,2,2,128]{4,2,1,0,3:T(2,128)} %rev.11) | copy-start | bytes 3072004
  116.2 1.2 copy-start.13
  116.6 1.3 copy-start.1
  116.6 1.6 %copy-start.2 = (f32[1000,1,2,128]{3,0,2,1:T(8,128)S(1)}, f32[1000,1,2,128]{3,0,2,1:T(8,128)}, u32[]{:S(2)}) copy-start(f32[1000,1,2,128]{3,0,2,1:T(8,128)} %get-tuple-element.77) | copy-start | bytes 3072004
  116.6 1.7 %copy-start.4 = (f32[1000,1,1,128]{3,0,2,1:T(8,128)S(1)}, f32[1000,1,1,128]{3,0,2,1:T(8,128)}, u32[]{:S(2)}) copy-start(f32[1000,1,1,128]{3,0,2,1:T(8,128)} %get-tuple-element.85) | copy-start | bytes 1536004
  116.6 1.9 %copy-start.5 = (f32[1000,1,1,128]{3,0,2,1:T(8,128)S(1)}, f32[1000,1,1,128]{3,0,2,1:T(8,128)}, u32[]{:S(2)}) copy-start(f32[1000,1,1,128]{3,0,2,1:T(8,128)} %get-tuple-element.86) | copy-start | bytes 1536004
  116.6 2.2 %copy-start.8 = (f32[1000,1,2,127]{3,0,2,1:T(8,128)S(1)}, f32[1000,1,2,127]{3,0,2,1:T(8,128)}, u32[]{:S(2)}) copy-start(f32[1000,1,2,127]{3,0,2,1:T(8,128)} %get-tuple-element.143) | copy-start | bytes 3048004
  116.6 2.5 %copy-start.9 = (f32[1000,1,2,127]{3,0,2,1:T(8,128)S(1)}, f32[1000,1,2,127]{3,0,2,1:T(8,128)}, u32[]{:S(2)}) copy-start(f32[1000,1,2,127]{3,0,2,1:T(8,128)} %get-tuple-element.144) | copy-start | bytes 3048004
  116.7 2.8 %copy-start.12 = (f32[1000,1,2,1]{3,0,2,1:T(8,128)S(1)}, f32[1000,1,2,1]{3,0,2,1:T(8,128)}, u32[]{:S(2)}) copy-start(f32[1000,1,2,1]{3,0,2,1:T(8,128)} %copy.144) | copy-start | bytes 24004
  119.4 1.5 %copy-start.6 = (f32[1000,1,2,127]{3,0,2,1:T(8,128)S(1)}, f32[1000,1,2,127]{3,0,2,1:T(8,128)}, u32[]{:S(2)}) copy-start(f32[1000,1,2,127]{3,0,2,1:T(8,128)} %get-tuple-element.99) | copy-start | bytes 3048004
  119.4 1.5 %copy-start.7 = (f32[1000,1,2,127]{3,0,2,1:T(8,128)S(1)}, f32[1000,1,2,127]{3,0,2,1:T(8,128)}, u32[]{:S(2)}) copy-start(f32[1000,1,2,127]{3,0,2,1:T(8,128)} %get-tuple-element.100) | copy-start | bytes 3048004
  119.4 1.8 %copy-start.10 = (f32[1000,1,2,1]{3,0,2,1:T(8,128)S(1)}, f32[1000,1,2,1]{3,0,2,1:T(8,128)}, u32[]{:S(2)}) copy-start(f32[1000,1,2,1]{3,0,2,1:T(8,128)} %copy.152) | copy-start | bytes 24004
  119.4 2.1 %copy-start.11 = (f32[1000,1,2,1]{3,0,2,1:T(8,128)S(1)}, f32[1000,1,2,1]{3,0,2,1:T(8,128)}, u32[]{:S(2)}) copy-start(f32[1000,1,2,1]{3,0,2,1:T(8,128)} %copy.151) | copy-start | bytes 24004
  121.6 1.5 %copy-start.18 = (f32[1000,1,1,128]{3,0,2,1:T(8,128)S(1)}, f32[1000,1,1,128]{3,0,2,1:T(8,128)}, u32[]{:S(2)}) copy-start(f32[1000,1,1,128]{3,0,2,1:T(8,128)} %get-tuple-element.95) | copy-start | bytes 1536004
  121.6 1.5 %copy-start.19 = (f32[1000,1,1,128]{3,0,2,1:T(8,128)S(1)}, f32[1000,1,1,128]{3,0,2,1:T(8,128)}, u32[]{:S(2)}) copy-start(f32[1000,1,1,128]{3,0,2,1:T(8,128)} %get-tuple-element.96) | copy-start | bytes 1536004
  123.0 1.9 %copy-start.3 = (f32[1000,3,2,128]{3,2,1,0:T(2,128)S(1)}, f32[1000,3,2,128]{3,2,1,0:T(2,128)}, u32[]{:S(2)}) copy-start(f32[1000,3,2,128]{3,2,1,0:T(2,128)} %param.5) | copy-start | bytes 9216004
Sparse Core Ops, SparseCore 0:
  39.8 54.3 all-reduce.1
where the time goes:
time: 137 us; the launch traced here: 136 us
  local copies, waits for them, and re-layouts  56.8 us (41%)
  other arithmetic  45.2 us (33%)
  between operations  13.9 us (10%)
  starting transfers between devices  10.5 us (8%)
  matrix products  9.19 us (7%)
    another operation x2, local copies, waits for them, and re-layouts, gauss_points(): jnp.stack([center + XI_SIGNS[q] * GAUSS * grad_x + ETA_SIGNS[q] * GAUSS *...  10.6 us
    dot_general x1, matrix products, shards(): jnp.dot(moment_rows, stacked, precision=lax.Precision.HIGHEST, preferred_...  9.19 us
    broadcast_in_dim x6, local copies, waits for them, and re-layouts, spread_pair(): jnp.broadcast_to(pieces[:, None], (pieces.shape[0], 2) + pieces.shape[1:])  8.75 us
    mul x1, other arithmetic, gauss_tangent(): gauss * (params[10] + rel_x * params[11] + rel_y * params[12] + rel_z * p...  7.97 us
    rev x3, local copies, waits for them, and re-layouts, partner(): return grouped[:, ::-1].reshape(dims_in)  7.74 us
    ppermute x2, starting transfers between devices, from_behind_2(): lax.ppermute(value, axis, [(source, source + steps) for source in range(i...  7.71 us
    unnamed x46, local copies, waits for them, and re-layouts  7.17 us
    concatenate x1, other arithmetic, shards(): jnp.concatenate([edge_rows[:, 1, :, None], grad_y[:, :, :-1]], axis=2)  5.76 us
  transfers between devices with their start and end apart: 5, of which 0 were waited for; matrix products, arithmetic and copies ran while one was open for 46% of the time, Pallas kernels for 0%

commit v1 on v0

v1 whole, which is shorter than its diff:
```python
import functools
import math

import jax
import jax.numpy as jnp
from jax import lax
from jax.experimental import pallas as pl
from jax.experimental.pallas import tpu as pltpu
from jax.sharding import PartitionSpec as P

NVX = 20
GAUSS = 0.5773502691896258
XI_SIGNS = (-1.0, -1.0, 1.0, 1.0)
ETA_SIGNS = (-1.0, 1.0, -1.0, 1.0)
DUOS = ((0, 0), (1, 1), (2, 2), (0, 1), (0, 2), (1, 2))
LOG_TWO_PI = math.log(2.0 * math.pi)
LOG2E = 1.0 / math.log(2.0)
HALF = NVX // 2
SPACING = 5.0 / HALF
UNIT = 0.5 * SPACING
FEATS = 16
SUB = 8
LANES = 128
CHUNK = 256
F32 = jnp.float32
BF16 = jnp.bfloat16
VMEM_LIMIT = 56 * 1024 * 1024


def roundup(value, unit):
    return -(-value // unit) * unit


def for_blocks(count, body, unroll):
    whole = count // SUB
    rounds = whole // unroll

    def step(i, carry):
        for k in range(unroll):
            body(pl.multiple_of((i * unroll + k) * SUB, SUB))
        return carry

    if rounds:
        lax.fori_loop(0, rounds, step, 0)
    for k in range(rounds * unroll, whole):
        body(k * SUB)
    if count % SUB:
        body(count - SUB)


def swap_pairs(value, low):
    return jnp.where(low, pltpu.roll(value, SUB - 2, 0), pltpu.roll(value, 2, 0))


def iota(shape, dim):
    return lax.broadcasted_iota(jnp.int32, shape, dim)


def towards():
    return jnp.where(lax.axis_index("gy") == 0, 1, -1)


def fill_features(feat, orient_ref, count):
    feat[...] = jnp.zeros(feat.shape, F32)
    slot = (iota((1, count), 1) + lax.axis_index("vert") * count).astype(F32)
    jz = jnp.floor((slot + 0.5) * (1.0 / (4 * HALF * HALF)))
    slot = slot - jz * (4.0 * HALF * HALF)
    mx = jnp.floor((slot + 0.5) * (1.0 / (4 * HALF)))
    slot = slot - mx * (4.0 * HALF)
    my = jnp.floor((slot + 0.5) * 0.25)
    sx = (2 * orient_ref[0:1, :] - 1).astype(F32)
    sy = (2 * orient_ref[1:2, :] - 1).astype(F32)
    ox = sx * (2.0 * mx + 1.0)
    oy = sy * (2.0 * my + 1.0)
    oz = 2.0 * jz - (2.0 * HALF - 1.0)
    cross = (ox * oy, ox * oz, oy * oz)
    high = [jnp.floor(c * 0.0625) * 16.0 for c in cross]
    low = [c - h for c, h in zip(cross, high)]
    rows = [jnp.ones_like(ox), ox, oy, oz, mx * (mx + 1.0), my * (my + 1.0), 0.25 * (oz * oz - 1.0)]
    rows = rows + high + low + [sx, sy, 2.0 * my + 1.0]
    for k, row in enumerate(rows):
        feat[k : k + 1, 0:count] = row


def spread_table(columns, step):
    rows = iota((LANES, LANES * len(columns)), 0)
    blocks = iota((LANES, LANES * len(columns)), 1) // LANES
    out = jnp.zeros(rows.shape, F32)
    for j, (row, scale) in enumerate(columns):
        out = jnp.where((rows == row) & (blocks == j), scale, out)
    return out.astype(BF16)


def pieces(value):
    high = value.astype(BF16)
    rest = value - high.astype(F32)
    mid = rest.astype(BF16)
    low = (rest - mid.astype(F32)).astype(BF16)
    return high, mid, low


def dot(left, right):
    return jnp.dot(left, right, preferred_element_type=F32)


def pre_kernel(count, rows, orient_ref, tan_hbm, st_hbm, ysend, xsend, mom, tab, feat, wide, edge, tan_v, st_v, sems):
    comps = 3 * rows
    padded = feat.shape[1]
    starts = list(range(0, padded, CHUNK))
    copies = []
    for a, (src, dst) in enumerate(((tan_hbm, tan_v), (st_hbm, st_v))):
        for j, start in enumerate(starts):
            size = min(CHUNK, count - start) * comps
            part = pl.ds(start * comps, size)
            copies.append(pltpu.make_async_copy(src.at[part], dst.at[part], sems.at[a * len(starts) + j]))
    for copy in copies:
        copy.start()
    tail = (padded - count) * comps
    for buf in (tan_v, st_v):
        if tail:
            buf[pl.ds(count * comps, tail), :] = jnp.zeros((tail, LANES), F32)
    edge[...] = jnp.zeros(edge.shape, F32)
    fill_features(feat, orient_ref, count)
    table = feat[...]
    spare = jnp.zeros((LANES - 3 * FEATS, padded), F32)
    flipped = jnp.concatenate([table, table, table, spare], axis=0).T.astype(BF16)
    tab[...] = flipped
    away = towards()
    scale = away.astype(F32)
    wide[...] = dot(flipped, spread_table([(13, 1.0), (14, 1.0)], 1))
    face = jnp.where(away == 1, rows - 1, 0)
    sub = iota((SUB, LANES), 0)
    low = sub % 4 < 2
    lane = iota((SUB, LANES), 1)
    for copy in copies[: len(starts)]:
        copy.wait()

    def pack(start):
        at = lambda comp, row: tan_v[pl.ds(start * comps + comp * rows + row, SUB, stride=comps), :]
        sx = wide[pl.ds(start, SUB), 0:LANES]
        sy = wide[pl.ds(start, SUB), LANES : 2 * LANES]
        center, grad_x, grad_y = at(0, face), at(1, face), at(2, face)
        out_y = center + sy * grad_y
        own = jnp.where(low, out_y, grad_x)
        other = jnp.where(low, grad_x, out_y)
        ysend[pl.ds(start, SUB), :] = jnp.where(sy * scale > 0.0, own, swap_pairs(other, low))
        right = sx > 0.0
        acc = jnp.zeros((SUB, LANES), F32)
        for row in range(rows):
            slope = at(2, row)
            value = at(0, row) + sx * at(1, row)
            for j, piece in ((2 * row, value), (2 * row + 1, slope)):
                here = jnp.where(right, pltpu.roll(piece, 1 + j, 1), pltpu.roll(piece, j, 1) if j else piece)
                acc = jnp.where(lane == j, here, acc)
        edge[pl.ds(start, SUB), :] = acc

    for_blocks(count, pack, 5)
    xsend[...] = edge[...].T[0 : xsend.shape[0], :]
    table = table.astype(BF16)
    for a, buf in enumerate((tan_v, st_v)):
        if a:
            for copy in copies[len(starts) :]:
                copy.wait()
        for c in range(comps):
            total = jnp.zeros((FEATS, LANES), F32)
            for start in starts:
                size = min(CHUNK, padded - start)
                data = buf[pl.ds(start * comps + c, size, stride=comps), :]
                high = data.astype(BF16)
                rest = (data - high.astype(F32)).astype(BF16)
                part = table[:, start : start + size]
                total = total + dot(part, high) + dot(part, rest)
            ones = total[0:1]
            squares = 4.0 * total[4:7] + ones
            cross = total[7:10] + total[10:13]
            slot = (1 - a) * comps + c
            mom[pl.ds(slot * 8, 4), :] = total[0:4]
            mom[pl.ds(slot * 8 + 4, 3), :] = squares
            mom[pl.ds(slot * 8 + 7, 1), :] = cross[0:1]
            mom[pl.ds(2 * comps * 8 + slot * 2, 2), :] = cross[1:3]


def transport_kernel(count, rows, cols, single, *refs):
    orient_ref, tan_v, tab, walls, behind = refs[:5]
    ahead = behind if single else refs[5]
    adv, wide = refs[-2:]
    comps = 3 * rows
    padded = tab.shape[0]
    away = towards()
    scale = away.astype(F32)
    right_row = jnp.concatenate([orient_ref[0:1, :], jnp.zeros((1, padded - count), jnp.int32)], axis=1) == 1
    arrived = jnp.where(right_row, behind[...], ahead[...])
    spare = jnp.zeros((LANES - 3 * SUB, padded), F32)
    parts = [piece.astype(F32) for piece in pieces(arrived)]
    edges = jnp.concatenate(parts + [spare], axis=0).T.astype(BF16)
    cols_w = [(1, UNIT), (2, UNIT), (15, UNIT), (13, 1.0), (14, scale)]
    wide[:, 0 : 5 * LANES] = dot(tab[...], spread_table(cols_w, 1))
    r = iota((LANES, LANES * 2 * rows), 0)
    b = iota((LANES, LANES * 2 * rows), 1) // LANES
    pick = jnp.where((r % SUB == b) & (r < 3 * SUB), 1.0, 0.0).astype(BF16)
    wide[:, 5 * LANES : (5 + 2 * rows) * LANES] = dot(edges, pick)
    sub = iota((SUB, LANES), 0)
    low = sub % 4 < 2
    lane = iota((SUB, LANES), 1)
    ends = jnp.where(lane == cols - 1, 1.0, 0.0) - jnp.where(lane == 0, 1.0, 0.0)
    wall_row = jnp.where(away == 1, walls[0:1, :], walls[1:2, :]).astype(F32)
    wall = jnp.broadcast_to(wall_row, (SUB, LANES))
    order = [jnp.where(away == 1, k, rows - 1 - k) for k in range(rows)]

    def block(start):
        at = lambda comp, row: tan_v[pl.ds(start * comps + comp * rows + row, SUB, stride=comps), :]
        col = lambda j: wide[pl.ds(start, SUB), j * LANES : (j + 1) * LANES]
        vx, vy, ay, sx, toward_sign = (col(j) for j in range(5))
        ax = vx * sx
        sy = toward_sign * scale
        right = sx > 0.0
        toward = toward_sign > 0.0
        outgoing = sx * ends > 0.0
        center = [at(0, order[k]) for k in range(rows)]
        grad_x = [at(1, order[k]) for k in range(rows)]
        grad_y = [at(2, order[k]) for k in range(rows)]
        out_y = [c + sy * g for c, g in zip(center, grad_y)]
        for k in range(rows):
            ecol = lambda j: wide[pl.ds(start, SUB), pl.ds(pl.multiple_of((5 + 2 * order[k] + j) * LANES, LANES), LANES)]
            out_x = center[k] + sx * grad_x[k]

            def inflow(piece, received):
                mixed = jnp.where(outgoing, received, piece)
                return jnp.where(right, pltpu.roll(mixed, 1, 1), pltpu.roll(mixed, cols - 1, 1))

            in_x = inflow(out_x, ecol(0))
            in_xs = inflow(grad_y[k], ecol(1))
            if k == 0:
                near_v = wall * swap_pairs(out_y[0], low)
                near_s = wall * swap_pairs(grad_x[0], low)
            else:
                near_v, near_s = out_y[k - 1], grad_x[k - 1]
            if k == rows - 1:
                far_v, far_s = jnp.zeros_like(near_v), jnp.zeros_like(near_s)
            else:
                far_v, far_s = out_y[k + 1], grad_x[k + 1]
            in_y = jnp.where(toward, near_v, far_v)
            in_ys = jnp.where(toward, near_s, far_s)
            twice = 2.0 * center[k]
            mean = ax * (out_x - in_x) + ay * (out_y[k] - in_y) + twice
            rate_x = 3.0 * vx * (out_x + in_x - twice) + ay * (grad_x[k] - in_ys) + 2.0 * grad_x[k]
            rate_y = ax * (grad_y[k] - in_xs) + 3.0 * vy * (out_y[k] + in_y - twice) + 2.0 * grad_y[k]
            for comp, value in enumerate((mean, rate_x, rate_y)):
                adv[pl.ds(start * comps + comp * rows + order[k], SUB, stride=comps), :] = value

    for_blocks(count, block, 2)


def sym(entries):
    grid = [[None] * 3 for _ in range(3)]
    for k, (i, j) in enumerate(DUOS):
        grid[i][j] = entries[k]
        grid[j][i] = entries[k]
    return grid


def point_params(moments):
    density = moments[0]
    inv_density = 1.0 / density
    u = [moments[1 + i] * inv_density for i in range(3)]
    second = [moments[4 + k] for k in range(6)]
    theta = [second[k] * inv_density - u[i] * u[j] for k, (i, j) in enumerate(DUOS)]
    temp = (theta[0] + theta[1] + theta[2]) / 3.0
    tensor = [(1.5 * temp if i == j else 0.0) - 0.5 * theta[k] for k, (i, j) in enumerate(DUOS)]
    t = sym(tensor)
    cof = [
        t[1][1] * t[2][2] - t[1][2] * t[1][2],
        t[0][0] * t[2][2] - t[0][2] * t[0][2],
        t[0][0] * t[1][1] - t[0][1] * t[0][1],
        t[0][2] * t[1][2] - t[0][1] * t[2][2],
        t[0][1] * t[1][2] - t[0][2] * t[1][1],
        t[0][1] * t[0][2] - t[0][0] * t[1][2],
    ]
    det = t[0][0] * cof[0] + t[0][1] * cof[3] + t[0][2] * cof[4]
    inv_det = 1.0 / det
    inverse = [entry * inv_det for entry in cof]
    log_pre = jnp.log(density) - 1.5 * LOG_TWO_PI - 0.5 * jnp.log(det)
    drho = moments[10]
    du = [(moments[11 + i] - u[i] * drho) * inv_density for i in range(3)]
    ratio = drho * inv_density
    dtheta = [
        moments[14 + k] * inv_density - second[k] * inv_density * ratio - (du[i] * u[j] + u[i] * du[j])
        for k, (i, j) in enumerate(DUOS)
    ]
    dtemp = (dtheta[0] + dtheta[1] + dtheta[2]) / 3.0
    dtensor = [(1.5 * dtemp if i == j else 0.0) - 0.5 * dtheta[k] for k, (i, j) in enumerate(DUOS)]
    a, d = sym(inverse), sym(dtensor)
    trace = sum(a[i][j] * d[j][i] for i in range(3) for j in range(3))
    shift = ratio - 0.5 * trace
    w = [a[i][0] * du[0] + a[i][1] * du[1] + a[i][2] * du[2] for i in range(3)]
    ad = [[a[i][0] * d[0][j] + a[i][1] * d[1][j] + a[i][2] * d[2][j] for j in range(3)] for i in range(3)]
    curve = [ad[i][0] * a[0][j] + ad[i][1] * a[1][j] + ad[i][2] * a[2][j] for i, j in DUOS]
    return u, inverse, log_pre, shift, w, curve


def feature_coefs(const, linear, quad):
    square = [UNIT * UNIT * quad[k] for k in range(6)]
    const = const + square[0] + square[1] + square[2]
    return [const] + [UNIT * l for l in linear] + [4.0 * s for s in square[:3]] + square[3:] + square[3:]


def collide_kernel(count, rows, mom, tab, adv, out, raw, turn, coef, power):
    comps = 3 * rows
    spots = 4 * rows
    weight = SPACING**3
    scales = [weight] + [weight * UNIT] * 3 + [weight * UNIT * UNIT] * 4
    row_scale = jnp.zeros((SUB, LANES), F32)
    sub = iota((SUB, LANES), 0)
    for k, s in enumerate(scales):
        row_scale = jnp.where(sub == k, s, row_scale)
    for a in range(2):
        for row in range(rows):
            first = [row_scale * mom[pl.ds((a * comps + c * rows + row) * 8, 8), :] for c in range(3)]
            last = [
                (weight * UNIT * UNIT) * mom[pl.ds(2 * comps * 8 + (a * comps + c * rows + row) * 2, 2), :]
                for c in range(3)
            ]
            for q in range(4):
                mix = lambda v: v[0] + (XI_SIGNS[q] * GAUSS) * v[1] + (ETA_SIGNS[q] * GAUSS) * v[2]
                base = (q * rows + row) * 24 + a * 10
                raw[pl.ds(base, 8), :] = mix(first)
                raw[pl.ds(base + 8, 2), :] = mix(last)
    moments = [raw[pl.ds(k, spots, stride=24), :] for k in range(20)]
    u, inverse, log_pre, shift, w, curve = point_params(moments)
    a, b = sym(inverse), sym(curve)
    au = [a[i][0] * u[0] + a[i][1] * u[1] + a[i][2] * u[2] for i in range(3)]
    bu = [b[i][0] * u[0] + b[i][1] * u[1] + b[i][2] * u[2] for i in range(3)]
    uau = u[0] * au[0] + u[1] * au[1] + u[2] * au[2]
    ubu = u[0] * bu[0] + u[1] * bu[1] + u[2] * bu[2]
    uw = u[0] * w[0] + u[1] * w[1] + u[2] * w[2]
    half = lambda m, k: (0.5 if k < 3 else 1.0) * m[k]
    expo = feature_coefs(
        LOG2E * (log_pre - 0.5 * uau),
        [LOG2E * v for v in au],
        [-LOG2E * half(inverse, k) for k in range(6)],
    )
    poly = feature_coefs(
        0.5 * (shift - uw + 0.5 * ubu),
        [0.5 * (w[i] - bu[i]) for i in range(3)],
        [0.5 * half(curve, k) for k in range(6)],
    )
    coef[...] = jnp.zeros(coef.shape, BF16)
    for p, entries in enumerate((expo, poly)):
        turn[...] = jnp.zeros(turn.shape, F32)
        for k, entry in enumerate(entries):
            turn[pl.ds(k * spots, spots), :] = entry
        for s in range(spots):
            lanes = pl.ds((p * spots + s) * LANES, LANES)
            for j, piece in enumerate(pieces(turn[pl.ds(s, FEATS, stride=spots), :])):
                coef[pl.ds(j * FEATS, FEATS), lanes] = piece
    root3 = 3.0 * GAUSS
    for start in range(0, count, CHUNK):
        size = min(CHUNK, count - start)
        power[...] = dot(tab[pl.ds(start, CHUNK), :], coef[...])

        def block(local):
            first = (start + local) * comps
            for row in range(rows):
                gd = []
                for q in range(4):
                    lane = (q * rows + row) * LANES
                    expo = power[pl.ds(local, SUB), lane : lane + LANES]
                    factor = power[pl.ds(local, SUB), spots * LANES + lane : spots * LANES + lane + LANES]
                    gd.append(jnp.exp2(expo) * factor)
                back, front = gd[0] + gd[1], gd[2] + gd[3]
                collided = (back + front, root3 * (front - back), root3 * ((gd[1] - gd[0]) + (gd[3] - gd[2])))
                for comp, value in enumerate(collided):
                    where = pl.ds(first + comp * rows + row, SUB, stride=comps)
                    out[where, :] = adv[where, :] - value

        for_blocks(size, block, 2)


def face_kernel(count, rows, col, tab, yrecv, out_hbm, out_v, wide, sems):
    comps = 3 * rows
    away = towards()
    scale = away.astype(F32)
    face = jnp.where(away == 1, rows - 1, 0)
    wide[...] = dot(tab[...], spread_table([(15, UNIT), (14, scale)], 1))
    low = iota((SUB, LANES), 0) % 4 < 2
    copies = []
    for j, start in enumerate(range(0, count, CHUNK)):
        size = min(CHUNK, count - start)
        part = pl.ds(start * comps, size * comps)
        out_v[part, :] = col[part, :]

        def block(local):
            at = start + local
            data = yrecv[pl.ds(at, SUB), :]
            turned = swap_pairs(data, low)
            speed = wide[pl.ds(at, SUB), 0:LANES]
            sign = wide[pl.ds(at, SUB), LANES : 2 * LANES]
            speed = jnp.where(sign < 0.0, speed, 0.0)
            value = speed * jnp.where(low, data, turned)
            slope = speed * jnp.where(low, turned, data)
            for comp, term in enumerate((value, slope, (3.0 * scale) * value)):
                where = pl.ds(at * comps + comp * rows + face, SUB, stride=comps)
                out_v[where, :] = col[where, :] - term

        for_blocks(size, block, 4)
        copies.append(pltpu.make_async_copy(out_v.at[part], out_hbm.at[part], sems.at[j]))
        copies[-1].start()
    for copy in copies:
        copy.wait()


def call(kernel, out_shape, scratch, ins, outs, name):
    return pl.pallas_call(
        kernel,
        out_shape=out_shape,
        in_specs=[pl.BlockSpec(memory_space=m) for m in ins],
        out_specs=jax.tree.map(lambda m: pl.BlockSpec(memory_space=m), outs),
        scratch_shapes=scratch,
        compiler_params=pltpu.CompilerParams(vmem_limit_bytes=VMEM_LIMIT),
        name=name,
    )


def exchange(value, axis, by):
    devices = lax.axis_size(axis)
    return lax.ppermute(value, axis, [(i, (i + by) % devices) for i in range(devices)])


def sum_over(value, axis):
    devices = lax.axis_size(axis)
    step = 1
    while step < devices:
        value = value + lax.ppermute(value, axis, [(i, i ^ step) for i in range(devices)])
        step *= 2
    return value


def shards(state, tangent, orient, walls):
    count, _, rows, cols = state.shape
    comps = 3 * rows
    total_rows = count * comps
    padded = roundup(count, CHUNK)
    chunks = padded // CHUNK
    st = state.reshape(total_rows, cols)
    tn = tangent.reshape(total_rows, cols)
    signs = orient.T
    vm, hbm = pltpu.VMEM, pl.ANY
    shape = jax.ShapeDtypeStruct
    ysend, xsend, mom, tab = call(
        functools.partial(pre_kernel, count, rows),
        (
            shape((count, cols), F32),
            shape((SUB, padded), F32),
            shape((2 * comps * 10, cols), F32),
            shape((padded, LANES), BF16),
        ),
        [
            pltpu.VMEM((FEATS, padded), F32),
            pltpu.VMEM((padded, 2 * LANES), F32),
            pltpu.VMEM((padded, LANES), F32),
            pltpu.VMEM((padded * comps, cols), F32),
            pltpu.VMEM((padded * comps, cols), F32),
            pltpu.SemaphoreType.DMA((2 * chunks,)),
        ],
        (vm, hbm, hbm),
        (vm, vm, vm, vm),
        "pack_and_moments",
    )(signs, tn, st)
    yrecv = lax.ppermute(ysend, "gy", [(0, 1), (1, 0)])
    single = lax.axis_size("gx") == 2
    behind = exchange(xsend, "gx", 1)
    edges = (behind,) if single else (behind, exchange(xsend, "gx", -1))
    mom = sum_over(mom, "vert")
    adv = call(
        functools.partial(transport_kernel, count, rows, cols, single),
        shape((total_rows, cols), F32),
        [pltpu.VMEM((padded, (5 + 2 * rows) * LANES), F32)],
        (vm,) * (4 + len(edges)),
        vm,
        "transport",
    )(signs, tn, tab, walls, *edges)
    col = call(
        functools.partial(collide_kernel, count, rows),
        shape((total_rows, cols), F32),
        [
            pltpu.VMEM((4 * rows * 24, LANES), F32),
            pltpu.VMEM((FEATS * 4 * rows, LANES), F32),
            pltpu.VMEM((LANES, 8 * rows * LANES), BF16),
            pltpu.VMEM((CHUNK, 8 * rows * LANES), F32),
        ],
        (vm, vm, vm),
        vm,
        "collide",
    )(mom, tab, adv)
    out = call(
        functools.partial(face_kernel, count, rows),
        shape((total_rows, cols), F32),
        [
            pltpu.VMEM((total_rows, cols), F32),
            pltpu.VMEM((padded, 2 * LANES), F32),
            pltpu.SemaphoreType.DMA((chunks,)),
        ],
        (vm, vm, vm),
        hbm,
        "faces",
    )(col, tab, yrecv)
    return out.reshape(state.shape)


def solution(mesh):
    placed = (
        P("vert", None, "gy", "gx"),
        P("vert", None, "gy", "gx"),
        P("vert", None),
        P(None, "gx"),
    )
    return jax.shard_map(
        shards, mesh=mesh, in_specs=placed, out_specs=P("vert", None, "gy", "gx"), check_vma=False
    )
```

time: 137 us -> 47 us (0.34)
  local copies, waits for them, and re-layouts: 56.8 us -> 1.38 us
  other arithmetic: 45.2 us -> 1.47 us
  Pallas kernels: 0 us -> 28.4 us
  between operations: 13.9 us -> 0.02 us
  matrix products: 9.19 us -> 0 us
  waiting for transfers between devices: 0.03 us -> 6.71 us
  starting transfers between devices: 10.5 us -> 8.74 us
    pallas_call x0 -> x4, Pallas kernels: none -> 28.4 us  [the longest x1 10.1 us: shards(): call(functools.partial(transport_kernel, count, rows, cols, single), shap...]
    another operation x8 -> x0, local copies, waits for them, and re-layouts: 15.3 us -> none  [the longest x2 10.6 us: gauss_points(): jnp.stack([center + XI_SIGNS[q] * GAUSS * grad_x + ETA_SIGNS[q] * GAUSS *...]
    mul x8 -> x0, other arithmetic: 9.45 us -> none  [the longest x1 7.97 us: gauss_tangent(): gauss * (params[10] + rel_x * params[11] + rel_y * params[12] + rel_z * p...]
    concatenate x4 -> x0, other arithmetic: 9.43 us -> none  [the longest x1 5.76 us: shards(): jnp.concatenate([edge_rows[:, 1, :, None], grad_y[:, :, :-1]], axis=2)]
    dot_general x1 -> x0, matrix products: 9.19 us -> none  [shards(): jnp.dot(moment_rows, stacked, precision=lax.Precision.HIGHEST, preferred_...]
    broadcast_in_dim x6 -> x0, local copies, waits for them, and re-layouts: 8.75 us -> none  [spread_pair(): jnp.broadcast_to(pieces[:, None], (pieces.shape[0], 2) + pieces.shape[1:])]
    rev x3 -> x0, local copies, waits for them, and re-layouts: 7.74 us -> none  [partner(): return grouped[:, ::-1].reshape(dims_in)]
    concatenate x7 -> x0, local copies, waits for them, and re-layouts: 6.85 us -> none  [the longest x1 1.45 us: shards(): jnp.concatenate([jnp.where(at_bottom, wall_part, field_part[:, 0])[:, Non...]
  transfers between devices with their start and end apart: 5 -> 5, of which waited for: 0 -> 3; matrix products, arithmetic and copies ran while one was open for 46% -> 3% of each run, Pallas kernels for 0% -> 36%
where the time goes in v1:
time: 47 us; the launch traced here: 46.7 us
  Pallas kernels  28.4 us (60%)
  starting transfers between devices  8.74 us (19%)
  waiting for transfers between devices  6.71 us (14%)
  other arithmetic  1.47 us (3%)
  local copies, waits for them, and re-layouts  1.38 us (3%)
    pallas_call x1, Pallas kernels, shards(): call(functools.partial(transport_kernel, count, rows, cols, single), shap...  10.1 us
    pallas_call x1, Pallas kernels, shards(): call(functools.partial(pre_kernel, count, rows), (shape((count, cols), F3...  7.28 us
    pallas_call x1, Pallas kernels, shards(): call(functools.partial(collide_kernel, count, rows), shape((total_rows, c...  6.88 us
    ppermute x3, starting transfers between devices, sum_over(): lax.ppermute(value, axis, [(i, i ^ step) for i in range(devices)])  4.23 us
    pallas_call x1, Pallas kernels, shards(): call(functools.partial(face_kernel, count, rows), shape((total_rows, cols...  4.13 us
    ppermute x3, waiting for transfers between devices, sum_over(): lax.ppermute(value, axis, [(i, i ^ step) for i in range(devices)])  4.1 us
    ppermute x1, starting transfers between devices, shards(): yrecv = lax.ppermute(ysend, 'gy', [(0, 1), (1, 0)])  2.99 us
    ppermute x1, waiting for transfers between devices, exchange(): lax.ppermute(value, axis, [(i, (i + by) % devices) for i in range(devices)])  2.61 us
  transfers between devices with their start and end apart: 5, of which 3 were waited for; matrix products, arithmetic and copies ran while one was open for 3% of the time, Pallas kernels for 36%

profile of v1, /device:TPU:0, one launch (start us, length us, event | category | flops | bytes accessed | tf_op | source)
XLA Modules:
  0.0 46.7 jit_solution(3196280456732939925)
XLA Ops:
  0.0 7.3 %pack_and_moments.1 = (f32[1000,128]{1,0:T(8,128)}, f32[8,1024]{1,0:T(8,128)}, f32[120,128]{1,0:T(8,128)}, bf16[1024,128]{1,0:T(8,128)(2,1)}) custom-call(s32[2,1000]{1,0:T(2,128)} %bitcast.7, f32[6000,128]{1,0:T(8,128)} %bitcast.4, f32[6000,128]{1,0:T(8,128)} %bitcast.6), custom_call_target="tpu_custom_call" | custom-call | tf_op jit(solution)/shard_map/pack_and_moments/pallas_call | solution.py:449
  7.3 3.0 %collective-permute-start.4 = (f32[1000,128]{1,0:T(8,128)}, f32[1000,128]{1,0:T(8,128)S(1)}, u32[]{:S(2)}, u32[]{:S(2)}) collective-permute-start(f32[1000,128]{1,0:T(8,128)} %get-tuple-element.12), channel_id=1, source_target_pairs={{0,8},{8,0},{1,9},{9,1},{2,10},{10,2},{3,11},{11,3},{4,12},{12,4},... | collective-permute-start | bytes 1536008 | tf_op jit(solution)/shard_map/ppermute | solution.py:469
  10.3 0.0 collective-permute-start
  10.3 1.5 %collective-permute-done = f32[120,128]{1,0:T(8,128)S(1)} collective-permute-done((f32[120,128]{1,0:T(8,128)}, f32[120,128]{1,0:T(8,128)S(1)}, u32[]{:S(2)}, u32[]{:S(2)}) %collective-permute-start) | collective-permute-done | bytes 61472 | tf_op jit(solution)/shard_map/ppermute | solution.py:433
  11.7 0.8 %add.9 = f32[120,128]{1,0:T(8,128)S(1)} add(f32[120,128]{1,0:T(8,128)} %get-tuple-element.9, f32[120,128]{1,0:T(8,128)S(1)} %collective-permute-done) | non-fusion elementwise | flops 15360 | bytes 184320 | tf_op jit(solution)/shard_map/add | solution.py:433
  12.6 1.6 %collective-permute-start.1 = (f32[120,128]{1,0:T(8,128)S(1)}, f32[120,128]{1,0:T(8,128)S(1)}, u32[]{:S(2)}, u32[]{:S(2)}) collective-permute-start(f32[120,128]{1,0:T(8,128)S(1)} %add.9), channel_id=1, source_target_pairs={{0,2},{1,3},{2,0},{3,1},{4,6},{5,7},{6,4},{7,5},{8,10},{9,11},{10,... | collective-permute-start | bytes 184328 | tf_op jit(solution)/shard_map/ppermute | solution.py:433
  14.2 2.6 %collective-permute-done.1 = f32[120,128]{1,0:T(8,128)S(1)} collective-permute-done((f32[120,128]{1,0:T(8,128)S(1)}, f32[120,128]{1,0:T(8,128)S(1)}, u32[]{:S(2)}, u32[]{:S(2)}) %collective-permute-start.1) | collective-permute-done | bytes 61472 | tf_op jit(solution)/shard_map/ppermute | solution.py:433
  16.8 2.7 %collective-permute-start.2 = (f32[120,128]{1,0:T(8,128)S(1)}, f32[120,128]{1,0:T(8,128)S(1)}, u32[]{:S(2)}, u32[]{:S(2)}) collective-permute-start(f32[120,128]{1,0:T(8,128)S(1)} %add.10), channel_id=1, source_target_pairs={{0,4},{1,5},{2,6},{3,7},{4,0},{5,1},{6,2},{7,3},{8,12},{9,13},{10,... | collective-permute-start | bytes 184328 | tf_op jit(solution)/shard_map/ppermute | solution.py:433
  19.5 1.5 %collective-permute-start.3 = (f32[8,1024]{1,0:T(8,128)}, f32[8,1024]{1,0:T(8,128)S(1)}, u32[]{:S(2)}, u32[]{:S(2)}) collective-permute-start(f32[8,1024]{1,0:T(8,128)} %get-tuple-element.11), channel_id=1, source_target_pairs={{0,16},{16,0},{1,17},{17,1},{2,18},{18,2},{3,19},{19,3},{4,20},{20... | collective-permute-start | bytes 98312 | tf_op jit(solution)/shard_map/ppermute | solution.py:426
  21.0 2.6 %collective-permute-done.3.refs_4_ = f32[8,1024]{1,0:T(8,128)S(1)} collective-permute-done((f32[8,1024]{1,0:T(8,128)}, f32[8,1024]{1,0:T(8,128)S(1)}, u32[]{:S(2)}, u32[]{:S(2)}) %collective-permute-start.3) | collective-permute-done | bytes 32800 | tf_op jit(solution)/shard_map/ppermute | solution.py:426
  23.6 0.0 copy-start.1
  23.6 0.6 %copy-done.1 = f32[8,1024]{1,0:T(8,128)} copy-done((f32[8,1024]{1,0:T(8,128)}, f32[8,1024]{1,0:T(8,128)S(1)}, u32[]{:S(2)}) %copy-start.1) | copy-done | bytes 32792
  24.2 10.1 %transport.1.adv = f32[6000,128]{1,0:T(8,128)} custom-call(s32[2,1000]{1,0:T(2,128)} %bitcast.8, f32[6000,128]{1,0:T(8,128)} %bitcast.5, bf16[1024,128]{1,0:T(8,128)(2,1)} %get-tuple-element.10.refs_2_.tab, s32[2,128]{1,0:T(2,128)} %refs_3_.1, f32[8,1024]{1,0:T(8,128)} %copy-done.1), custom_call_target="tpu_custom_call" | custom-call | tf_op jit(solution)/shard_map/transport/pallas_call | solution.py:474
  34.3 0.0 collective-permute-done.2
  34.3 0.6 %add.11.mom = f32[120,128]{1,0:T(8,128)} add(f32[120,128]{1,0:T(8,128)S(1)} %add.10, f32[120,128]{1,0:T(8,128)S(1)} %collective-permute-done.2) | non-fusion elementwise | flops 15360 | bytes 184320 | tf_op jit(solution)/shard_map/add | solution.py:433
  34.9 6.9 %collide.1.col = f32[6000,128]{1,0:T(8,128)} custom-call(f32[120,128]{1,0:T(8,128)} %add.11.mom, bf16[1024,128]{1,0:T(8,128)(2,1)} %get-tuple-element.10.refs_2_.tab, f32[6000,128]{1,0:T(8,128)} %transport.1.adv), custom_call_target="tpu_custom_call" | custom-call | tf_op jit(solution)/shard_map/collide/pallas_call | solution.py:482
  41.8 0.0 collective-permute-done.4.yrecv
  41.8 0.0 copy-start
  41.8 0.8 %copy-done = f32[1000,128]{1,0:T(8,128)} copy-done((f32[1000,128]{1,0:T(8,128)}, f32[1000,128]{1,0:T(8,128)S(1)}, u32[]{:S(2)}) %copy-start) | copy-done | bytes 512024
  42.6 4.1 %faces.1 = f32[6000,128]{1,0:T(8,128)} custom-call(f32[6000,128]{1,0:T(8,128)} %collide.1.col, bf16[1024,128]{1,0:T(8,128)(2,1)} %get-tuple-element.10.refs_2_.tab, f32[1000,128]{1,0:T(8,128)} %copy-done), custom_call_target="tpu_custom_call" | custom-call | tf_op jit(solution)/shard_map/faces/pallas_call | solution.py:495
  (1 shorter events, 0.0 us)
Async XLA Ops:
  7.3 34.5 %collective-permute-start.4 = (f32[1000,128]{1,0:T(8,128)}, f32[1000,128]{1,0:T(8,128)S(1)}, u32[]{:S(2)}, u32[]{:S(2)}) collective-permute-start(f32[1000,128]{1,0:T(8,128)} %get-tuple-element.12), channel_id=1, source_target_pairs={{0,8},{8,0},{1,9},{9,1},{2,10},{10,2},{3,11},{11,3},{4,12},{12,4},... | collective-permute-start | bytes 1536008 | tf_op jit(solution)/shard_map/ppermute | solution.py:469
  10.3 1.5 %collective-permute-start = (f32[120,128]{1,0:T(8,128)}, f32[120,128]{1,0:T(8,128)S(1)}, u32[]{:S(2)}, u32[]{:S(2)}) collective-permute-start(f32[120,128]{1,0:T(8,128)} %get-tuple-element.9), channel_id=1, source_target_pairs={{0,1},{1,0},{2,3},{3,2},{4,5},{5,4},{6,7},{7,6},{8,9},{9,8},{10,11... | collective-permute-start | bytes 184328 | tf_op jit(solution)/shard_map/ppermute | solution.py:433
  12.6 4.2 %collective-permute-start.1 = (f32[120,128]{1,0:T(8,128)S(1)}, f32[120,128]{1,0:T(8,128)S(1)}, u32[]{:S(2)}, u32[]{:S(2)}) collective-permute-start(f32[120,128]{1,0:T(8,128)S(1)} %add.9), channel_id=1, source_target_pairs={{0,2},{1,3},{2,0},{3,1},{4,6},{5,7},{6,4},{7,5},{8,10},{9,11},{10,... | collective-permute-start | bytes 184328 | tf_op jit(solution)/shard_map/ppermute | solution.py:433
  16.8 17.5 %collective-permute-start.2 = (f32[120,128]{1,0:T(8,128)S(1)}, f32[120,128]{1,0:T(8,128)S(1)}, u32[]{:S(2)}, u32[]{:S(2)}) collective-permute-start(f32[120,128]{1,0:T(8,128)S(1)} %add.10), channel_id=1, source_target_pairs={{0,4},{1,5},{2,6},{3,7},{4,0},{5,1},{6,2},{7,3},{8,12},{9,13},{10,... | collective-permute-start | bytes 184328 | tf_op jit(solution)/shard_map/ppermute | solution.py:433
  19.5 4.1 %collective-permute-start.3 = (f32[8,1024]{1,0:T(8,128)}, f32[8,1024]{1,0:T(8,128)S(1)}, u32[]{:S(2)}, u32[]{:S(2)}) collective-permute-start(f32[8,1024]{1,0:T(8,128)} %get-tuple-element.11), channel_id=1, source_target_pairs={{0,16},{16,0},{1,17},{17,1},{2,18},{18,2},{3,19},{19,3},{4,20},{20... | collective-permute-start | bytes 98312 | tf_op jit(solution)/shard_map/ppermute | solution.py:426
  23.6 0.6 %copy-start.1 = (f32[8,1024]{1,0:T(8,128)}, f32[8,1024]{1,0:T(8,128)S(1)}, u32[]{:S(2)}) copy-start(f32[8,1024]{1,0:T(8,128)S(1)} %collective-permute-done.3.refs_4_) | copy-start | bytes 98308
  41.8 0.8 %copy-start = (f32[1000,128]{1,0:T(8,128)}, f32[1000,128]{1,0:T(8,128)S(1)}, u32[]{:S(2)}) copy-start(f32[1000,128]{1,0:T(8,128)S(1)} %collective-permute-done.4.yrecv) | copy-start | bytes 1536004

commit v2 on v1

--- a/solution.py
+++ b/solution.py
@@ -22,9 +22,10 @@
 SUB = 8
 LANES = 128
 CHUNK = 256
+U_PACK, U_TRANS, U_COLL, U_FACE = 25, 16, 16, 32
 F32 = jnp.float32
 BF16 = jnp.bfloat16
-VMEM_LIMIT = 56 * 1024 * 1024
+VMEM_LIMIT = 16 * 1024 * 1024
 
 
 def roundup(value, unit):
@@ -35,17 +36,21 @@
     whole = count // SUB
     rounds = whole // unroll
 
+    def group(firsts):
+        for ref, where, value in [store for first in firsts for store in body(first)]:
+            ref[where] = value
+
     def step(i, carry):
-        for k in range(unroll):
-            body(pl.multiple_of((i * unroll + k) * SUB, SUB))
+        group([pl.multiple_of((i * unroll + k) * SUB, SUB) for k in range(unroll)])
         return carry
 
     if rounds:
         lax.fori_loop(0, rounds, step, 0)
-    for k in range(rounds * unroll, whole):
-        body(k * SUB)
+    left = [k * SUB for k in range(rounds * unroll, whole)]
+    if left:
+        group(left)
     if count % SUB:
-        body(count - SUB)
+        group([count - SUB])
 
 
 def swap_pairs(value, low):
@@ -103,7 +108,7 @@
     return jnp.dot(left, right, preferred_element_type=F32)
 
 
-def pre_kernel(count, rows, orient_ref, tan_hbm, st_hbm, ysend, xsend, mom, tab, feat, wide, edge, tan_v, st_v, sems):
+def pre_kernel(count, rows, orient_hbm, tan_hbm, st_hbm, ysend, xsend, mom, tab, tan_v, orient_ref, feat, wide, edge, st_v, sems):
     comps = 3 * rows
     padded = feat.shape[1]
     starts = list(range(0, padded, CHUNK))
@@ -113,6 +118,8 @@
             size = min(CHUNK, count - start) * comps
             part = pl.ds(start * comps, size)
             copies.append(pltpu.make_async_copy(src.at[part], dst.at[part], sems.at[a * len(starts) + j]))
+    signs = pltpu.make_async_copy(orient_hbm, orient_ref, sems.at[2 * len(starts)])
+    signs.start()
     for copy in copies:
         copy.start()
     tail = (padded - count) * comps
@@ -120,6 +127,7 @@
         if tail:
             buf[pl.ds(count * comps, tail), :] = jnp.zeros((tail, LANES), F32)
     edge[...] = jnp.zeros(edge.shape, F32)
+    signs.wait()
     fill_features(feat, orient_ref, count)
     table = feat[...]
     spare = jnp.zeros((LANES - 3 * FEATS, padded), F32)
@@ -143,7 +151,7 @@
         out_y = center + sy * grad_y
         own = jnp.where(low, out_y, grad_x)
         other = jnp.where(low, grad_x, out_y)
-        ysend[pl.ds(start, SUB), :] = jnp.where(sy * scale > 0.0, own, swap_pairs(other, low))
+        packed = jnp.where(sy * scale > 0.0, own, swap_pairs(other, low))
         right = sx > 0.0
         acc = jnp.zeros((SUB, LANES), F32)
         for row in range(rows):
@@ -152,9 +160,10 @@
             for j, piece in ((2 * row, value), (2 * row + 1, slope)):
                 here = jnp.where(right, pltpu.roll(piece, 1 + j, 1), pltpu.roll(piece, j, 1) if j else piece)
                 acc = jnp.where(lane == j, here, acc)
-        edge[pl.ds(start, SUB), :] = acc
-
-    for_blocks(count, pack, 5)
+        where = (pl.ds(start, SUB), slice(None))
+        return [(ysend, where, packed), (edge, where, acc)]
+
+    for_blocks(count, pack, U_PACK)
     xsend[...] = edge[...].T[0 : xsend.shape[0], :]
     table = table.astype(BF16)
     for a, buf in enumerate((tan_v, st_v)):
@@ -181,15 +190,18 @@
 
 
 def transport_kernel(count, rows, cols, single, *refs):
-    orient_ref, tan_v, tab, walls, behind = refs[:5]
-    ahead = behind if single else refs[5]
+    tan_v, tab, walls, behind = refs[:4]
     adv, wide = refs[-2:]
     comps = 3 * rows
     padded = tab.shape[0]
     away = towards()
     scale = away.astype(F32)
-    right_row = jnp.concatenate([orient_ref[0:1, :], jnp.zeros((1, padded - count), jnp.int32)], axis=1) == 1
-    arrived = jnp.where(right_row, behind[...], ahead[...])
+    arrived = behind[...]
+    if not single:
+        ahead, signs = refs[4:6]
+        spare = [jnp.zeros((1, padded - count), jnp.int32)] if padded > count else []
+        right_row = jnp.concatenate([signs[0:1, :]] + spare, axis=1) == 1
+        arrived = jnp.where(right_row, arrived, ahead[...])
     spare = jnp.zeros((LANES - 3 * SUB, padded), F32)
     parts = [piece.astype(F32) for piece in pieces(arrived)]
     edges = jnp.concatenate(parts + [spare], axis=0).T.astype(BF16)
@@ -220,6 +232,7 @@
         grad_x = [at(1, order[k]) for k in range(rows)]
         grad_y = [at(2, order[k]) for k in range(rows)]
         out_y = [c + sy * g for c, g in zip(center, grad_y)]
+        stores = []
         for k in range(rows):
             ecol = lambda j: wide[pl.ds(start, SUB), pl.ds(pl.multiple_of((5 + 2 * order[k] + j) * LANES, LANES), LANES)]
             out_x = center[k] + sx * grad_x[k]
@@ -246,9 +259,11 @@
             rate_x = 3.0 * vx * (out_x + in_x - twice) + ay * (grad_x[k] - in_ys) + 2.0 * grad_x[k]
             rate_y = ax * (grad_y[k] - in_xs) + 3.0 * vy * (out_y[k] + in_y - twice) + 2.0 * grad_y[k]
             for comp, value in enumerate((mean, rate_x, rate_y)):
-                adv[pl.ds(start * comps + comp * rows + order[k], SUB, stride=comps), :] = value
-
-    for_blocks(count, block, 2)
+                where = pl.ds(start * comps + comp * rows + order[k], SUB, stride=comps)
+                stores.append((adv, (where, slice(None)), value))
+        return stores
+
+    for_blocks(count, block, U_TRANS)
 
 
 def sym(entries):
@@ -360,6 +375,7 @@
 
         def block(local):
             first = (start + local) * comps
+            stores = []
             for row in range(rows):
                 gd = []
                 for q in range(4):
@@ -371,9 +387,10 @@
                 collided = (back + front, root3 * (front - back), root3 * ((gd[1] - gd[0]) + (gd[3] - gd[2])))
                 for comp, value in enumerate(collided):
                     where = pl.ds(first + comp * rows + row, SUB, stride=comps)
-                    out[where, :] = adv[where, :] - value
-
-        for_blocks(size, block, 2)
+                    stores.append((out, (where, slice(None)), adv[where, :] - value))
+            return stores
+
+        for_blocks(size, block, U_COLL)
 
 
 def face_kernel(count, rows, col, tab, yrecv, out_hbm, out_v, wide, sems):
@@ -398,11 +415,13 @@
             speed = jnp.where(sign < 0.0, speed, 0.0)
             value = speed * jnp.where(low, data, turned)
             slope = speed * jnp.where(low, turned, data)
+            stores = []
             for comp, term in enumerate((value, slope, (3.0 * scale) * value)):
                 where = pl.ds(at * comps + comp * rows + face, SUB, stride=comps)
-                out_v[where, :] = col[where, :] - term
-
-        for_blocks(size, block, 4)
+                stores.append((out_v, (where, slice(None)), col[where, :] - term))
+            return stores
+
+        for_blocks(size, block, U_FACE)
         copies.append(pltpu.make_async_copy(out_v.at[part], out_hbm.at[part], sems.at[j]))
         copies[-1].start()
     for copy in copies:
@@ -426,13 +445,15 @@
     return lax.ppermute(value, axis, [(i, (i + by) % devices) for i in range(devices)])
 
 
-def sum_over(value, axis):
+def sum_over(value, axis, beside):
     devices = lax.axis_size(axis)
     step = 1
     while step < devices:
+        if step == 4:
+            value, *beside = lax.optimization_barrier((value, *beside))
         value = value + lax.ppermute(value, axis, [(i, i ^ step) for i in range(devices)])
         step *= 2
-    return value
+    return value, beside
 
 
 def shards(state, tangent, orient, walls):
@@ -444,41 +465,43 @@
     st = state.reshape(total_rows, cols)
     tn = tangent.reshape(total_rows, cols)
     signs = orient.T
-    vm, hbm = pltpu.VMEM, pl.ANY
+    hold = [pltpu.with_memory_space_constraint(v, pltpu.HBM) for v in (signs, tn, st)]
+    vm, hbm = pltpu.VMEM, pltpu.HBM
     shape = jax.ShapeDtypeStruct
-    ysend, xsend, mom, tab = call(
+    ysend, xsend, mom, tab, tan_v = call(
         functools.partial(pre_kernel, count, rows),
         (
             shape((count, cols), F32),
             shape((SUB, padded), F32),
             shape((2 * comps * 10, cols), F32),
             shape((padded, LANES), BF16),
+            shape((padded * comps, cols), F32),
         ),
         [
+            pltpu.VMEM((2, count), jnp.int32),
             pltpu.VMEM((FEATS, padded), F32),
             pltpu.VMEM((padded, 2 * LANES), F32),
             pltpu.VMEM((padded, LANES), F32),
             pltpu.VMEM((padded * comps, cols), F32),
-            pltpu.VMEM((padded * comps, cols), F32),
-            pltpu.SemaphoreType.DMA((2 * chunks,)),
+            pltpu.SemaphoreType.DMA((2 * chunks + 1,)),
         ],
-        (vm, hbm, hbm),
-        (vm, vm, vm, vm),
+        (hbm, hbm, hbm),
+        (vm, vm, vm, vm, vm),
         "pack_and_moments",
-    )(signs, tn, st)
+    )(*hold)
     yrecv = lax.ppermute(ysend, "gy", [(0, 1), (1, 0)])
     single = lax.axis_size("gx") == 2
-    behind = exchange(xsend, "gx", 1)
-    edges = (behind,) if single else (behind, exchange(xsend, "gx", -1))
-    mom = sum_over(mom, "vert")
+    edges = (exchange(xsend, "gx", 1),) + (() if single else (exchange(xsend, "gx", -1),))
+    mom, edges = sum_over(mom, "vert", edges)
+    edges += [] if single else [signs]
     adv = call(
         functools.partial(transport_kernel, count, rows, cols, single),
         shape((total_rows, cols), F32),
         [pltpu.VMEM((padded, (5 + 2 * rows) * LANES), F32)],
-        (vm,) * (4 + len(edges)),
+        (vm,) * (3 + len(edges)),
         vm,
         "transport",
-    )(signs, tn, tab, walls, *edges)
+    )(tan_v, tab, walls, *edges)
     col = call(
         functools.partial(collide_kernel, count, rows),
         shape((total_rows, cols), F32),

time: 47 us -> 24.7 us (0.53)
  Pallas kernels: 28.4 us -> 11.6 us
  waiting for transfers between devices: 6.71 us -> 4.1 us
  other arithmetic: 1.47 us -> 0.03 us
  local copies, waits for them, and re-layouts: 1.38 us -> 0.01 us
    pallas_call x1, Pallas kernels: 10.1 us -> 2.6 us  [shards(): call(functools.partial(transport_kernel, count, rows, cols, single), shap...]
    pallas_call x1, Pallas kernels: 6.88 us -> 2.61 us  [shards(): call(functools.partial(collide_kernel, count, rows), shape((total_rows, c...]
    pallas_call x1, Pallas kernels: 7.28 us -> 4.46 us  [shards(): call(functools.partial(pre_kernel, count, rows), (shape((count, cols), F3...]
    pallas_call x1, Pallas kernels: 4.13 us -> 1.96 us  [shards(): call(functools.partial(face_kernel, count, rows), shape((total_rows, cols...]
    add x3, other arithmetic: 1.47 us -> 0.03 us  [sum_over(): value + lax.ppermute(value, axis, [(i, i ^ step) for i in range(devices)])]
    unnamed x4 -> x2, local copies, waits for them, and re-layouts: 1.38 us -> 0.01 us
    ppermute x1, waiting for transfers between devices: 2.61 us -> 1.26 us  [exchange(): lax.ppermute(value, axis, [(i, (i + by) % devices) for i in range(devices)])]
    ppermute x3, waiting for transfers between devices: 4.1 us -> 2.84 us  [sum_over(): lax.ppermute(value, axis, [(i, i ^ step) for i in range(devices)])]
  transfers between devices with their start and end apart: 5 -> 5, of which waited for: 3 -> 4; matrix products, arithmetic and copies ran while one was open for 3% -> 0% of each run, Pallas kernels for 36% -> 21%
where the time goes in v2:
time: 24.7 us; the launch traced here: 24.5 us
  Pallas kernels  11.6 us (47%)
  starting transfers between devices  8.72 us (35%)
  waiting for transfers between devices  4.1 us (17%)
    pallas_call x1, Pallas kernels, shards(): call(functools.partial(pre_kernel, count, rows), (shape((count, cols), F3...  4.46 us
    ppermute x3, starting transfers between devices, sum_over(): lax.ppermute(value, axis, [(i, i ^ step) for i in range(devices)])  4.23 us
    ppermute x1, starting transfers between devices, shards(): yrecv = lax.ppermute(ysend, 'gy', [(0, 1), (1, 0)])  2.97 us
    ppermute x3, waiting for transfers between devices, sum_over(): lax.ppermute(value, axis, [(i, i ^ step) for i in range(devices)])  2.84 us
    pallas_call x1, Pallas kernels, shards(): call(functools.partial(collide_kernel, count, rows), shape((total_rows, c...  2.61 us
    pallas_call x1, Pallas kernels, shards(): call(functools.partial(transport_kernel, count, rows, cols, single), shap...  2.6 us
    pallas_call x1, Pallas kernels, shards(): call(functools.partial(face_kernel, count, rows), shape((total_rows, cols...  1.96 us
    ppermute x1, starting transfers between devices, exchange(): lax.ppermute(value, axis, [(i, (i + by) % devices) for i in range(devices)])  1.52 us
  transfers between devices with their start and end apart: 5, of which 4 were waited for; matrix products, arithmetic and copies ran while one was open for 0% of the time, Pallas kernels for 21%

profile of v2, /device:TPU:0, one launch (start us, length us, event | category | flops | bytes accessed | tf_op | source)
XLA Modules:
  0.0 24.5 jit_solution(4716934530541859959)
XLA Ops:
  0.0 0.0 copy-start
  0.0 4.5 %pack_and_moments.1 = (f32[1000,128]{1,0:T(8,128)S(1)}, f32[8,1024]{1,0:T(8,128)S(1)}, f32[120,128]{1,0:T(8,128)S(1)}, bf16[1024,128]{1,0:T(8,128)(2,1)S(1)}, f32[6144,128]{1,0:T(8,128)S(1)}) custom-call(s32[2,1000]{1,0:T(2,128)} %bitcast.6, f32[6000,128]{1,0:T(8,128)} %bitcast.4, f32[6000,128]{1,0:T(8,128)} %bitcast.5), custom_call_target="tpu_custom_call" | custom-call | tf_op jit(solution)/shard_map/pack_and_moments/pallas_call | solution.py:471
  4.5 3.0 %collective-permute-start.4 = (f32[1000,128]{1,0:T(8,128)S(1)}, f32[1000,128]{1,0:T(8,128)S(1)}, u32[]{:S(2)}, u32[]{:S(2)}) collective-permute-start(f32[1000,128]{1,0:T(8,128)S(1)} %get-tuple-element.18), channel_id=1, source_target_pairs={{0,8},{8,0},{1,9},{9,1},{2,10},{10,2},{3,11},{11,3},{4,12},{12,4},... | collective-permute-start | bytes 1536008 | tf_op jit(solution)/shard_map/ppermute | solution.py:492
  7.4 0.0 collective-permute-start
  7.4 1.2 %collective-permute-done = f32[120,128]{1,0:T(8,128)S(1)} collective-permute-done((f32[120,128]{1,0:T(8,128)S(1)}, f32[120,128]{1,0:T(8,128)S(1)}, u32[]{:S(2)}, u32[]{:S(2)}) %collective-permute-start) | collective-permute-done | bytes 61472 | tf_op jit(solution)/shard_map/ppermute | solution.py:454
  8.7 1.6 %collective-permute-start.1 = (f32[120,128]{1,0:T(8,128)S(1)}, f32[120,128]{1,0:T(8,128)S(1)}, u32[]{:S(2)}, u32[]{:S(2)}) collective-permute-start(f32[120,128]{1,0:T(8,128)S(1)} %add.9), channel_id=1, source_target_pairs={{0,2},{1,3},{2,0},{3,1},{4,6},{5,7},{6,4},{7,5},{8,10},{9,11},{10,... | collective-permute-start | bytes 184328 | tf_op jit(solution)/shard_map/ppermute | solution.py:454
  10.3 1.5 %collective-permute-start.2 = (f32[8,1024]{1,0:T(8,128)S(1)}, f32[8,1024]{1,0:T(8,128)S(1)}, u32[]{:S(2)}, u32[]{:S(2)}) collective-permute-start(f32[8,1024]{1,0:T(8,128)S(1)} %get-tuple-element.13), channel_id=1, source_target_pairs={{0,16},{16,0},{1,17},{17,1},{2,18},{18,2},{3,19},{19,3},{4,20},{20... | collective-permute-start | bytes 98312 | tf_op jit(solution)/shard_map/ppermute | solution.py:445
  11.9 1.1 %collective-permute-done.1 = f32[120,128]{1,0:T(8,128)S(1)} collective-permute-done((f32[120,128]{1,0:T(8,128)S(1)}, f32[120,128]{1,0:T(8,128)S(1)}, u32[]{:S(2)}, u32[]{:S(2)}) %collective-permute-start.1) | collective-permute-done | bytes 61472 | tf_op jit(solution)/shard_map/ppermute | solution.py:454
  13.0 1.3 %collective-permute-done.2.refs_3_ = f32[8,1024]{1,0:T(8,128)S(1)} collective-permute-done((f32[8,1024]{1,0:T(8,128)S(1)}, f32[8,1024]{1,0:T(8,128)S(1)}, u32[]{:S(2)}, u32[]{:S(2)}) %collective-permute-start.2) | collective-permute-done | bytes 32800 | tf_op jit(solution)/shard_map/ppermute | solution.py:445
  14.3 2.6 %collective-permute-start.3 = (f32[120,128]{1,0:T(8,128)S(1)}, f32[120,128]{1,0:T(8,128)S(1)}, u32[]{:S(2)}, u32[]{:S(2)}) collective-permute-start(f32[120,128]{1,0:T(8,128)S(1)} %add.10), channel_id=1, source_target_pairs={{0,4},{1,5},{2,6},{3,7},{4,0},{5,1},{6,2},{7,3},{8,12},{9,13},{10,... | collective-permute-start | bytes 184328 | tf_op jit(solution)/shard_map/ppermute | solution.py:454
  16.8 0.0 copy-done
  16.8 2.6 %transport.1.adv = f32[6000,128]{1,0:T(8,128)S(1)} custom-call(f32[6144,128]{1,0:T(8,128)S(1)} %get-tuple-element.16.refs_0_, bf16[1024,128]{1,0:T(8,128)(2,1)S(1)} %get-tuple-element.15.refs_1_.tab, s32[2,128]{1,0:T(2,128)S(1)} %copy-done, f32[8,1024]{1,0:T(8,128)S(1)} %collective-permute-done.2.refs_3_), custom_call_target="tpu_custom_call" | custom-call | tf_op jit(solution)/shard_map/transport/pallas_call | solution.py:497
  19.5 0.5 %collective-permute-done.3 = f32[120,128]{1,0:T(8,128)S(1)} collective-permute-done((f32[120,128]{1,0:T(8,128)S(1)}, f32[120,128]{1,0:T(8,128)S(1)}, u32[]{:S(2)}, u32[]{:S(2)}) %collective-permute-start.3) | collective-permute-done | bytes 61472 | tf_op jit(solution)/shard_map/ppermute | solution.py:454
  19.9 2.6 %collide.1.col = f32[6000,128]{1,0:T(8,128)S(1)} custom-call(f32[120,128]{1,0:T(8,128)S(1)} %add.11.mom, bf16[1024,128]{1,0:T(8,128)(2,1)S(1)} %get-tuple-element.15.refs_1_.tab, f32[6000,128]{1,0:T(8,128)S(1)} %transport.1.adv), custom_call_target="tpu_custom_call" | custom-call | tf_op jit(solution)/shard_map/collide/pallas_call | solution.py:505
  22.5 0.0 collective-permute-done.4.yrecv
  22.6 2.0 %faces.1 = f32[6000,128]{1,0:T(8,128)} custom-call(f32[6000,128]{1,0:T(8,128)S(1)} %collide.1.col, bf16[1024,128]{1,0:T(8,128)(2,1)S(1)} %get-tuple-element.15.refs_1_.tab, f32[1000,128]{1,0:T(8,128)S(1)} %collective-permute-done.4.yrecv), custom_call_target="tpu_custom_call" | custom-call | tf_op jit(solution)/shard_map/faces/pallas_call | solution.py:518
  (3 shorter events, 0.0 us)
Async XLA Ops:
  0.0 16.8 %copy-start = (s32[2,128]{1,0:T(2,128)S(1)}, s32[2,128]{1,0:T(2,128)}, u32[]{:S(2)}) copy-start(s32[2,128]{1,0:T(2,128)} %refs_2_.1) | copy-start | bytes 3076
  4.5 18.1 %collective-permute-start.4 = (f32[1000,128]{1,0:T(8,128)S(1)}, f32[1000,128]{1,0:T(8,128)S(1)}, u32[]{:S(2)}, u32[]{:S(2)}) collective-permute-start(f32[1000,128]{1,0:T(8,128)S(1)} %get-tuple-element.18), channel_id=1, source_target_pairs={{0,8},{8,0},{1,9},{9,1},{2,10},{10,2},{3,11},{11,3},{4,12},{12,4},... | collective-permute-start | bytes 1536008 | tf_op jit(solution)/shard_map/ppermute | solution.py:492
  7.4 1.2 %collective-permute-start = (f32[120,128]{1,0:T(8,128)S(1)}, f32[120,128]{1,0:T(8,128)S(1)}, u32[]{:S(2)}, u32[]{:S(2)}) collective-permute-start(f32[120,128]{1,0:T(8,128)S(1)} %get-tuple-element.12), channel_id=1, source_target_pairs={{0,1},{1,0},{2,3},{3,2},{4,5},{5,4},{6,7},{7,6},{8,9},{9,8},{10,11... | collective-permute-start | bytes 184328 | tf_op jit(solution)/shard_map/ppermute | solution.py:454
  8.7 4.3 %collective-permute-start.1 = (f32[120,128]{1,0:T(8,128)S(1)}, f32[120,128]{1,0:T(8,128)S(1)}, u32[]{:S(2)}, u32[]{:S(2)}) collective-permute-start(f32[120,128]{1,0:T(8,128)S(1)} %add.9), channel_id=1, source_target_pairs={{0,2},{1,3},{2,0},{3,1},{4,6},{5,7},{6,4},{7,5},{8,10},{9,11},{10,... | collective-permute-start | bytes 184328 | tf_op jit(solution)/shard_map/ppermute | solution.py:454
  10.3 3.9 %collective-permute-start.2 = (f32[8,1024]{1,0:T(8,128)S(1)}, f32[8,1024]{1,0:T(8,128)S(1)}, u32[]{:S(2)}, u32[]{:S(2)}) collective-permute-start(f32[8,1024]{1,0:T(8,128)S(1)} %get-tuple-element.13), channel_id=1, source_target_pairs={{0,16},{16,0},{1,17},{17,1},{2,18},{18,2},{3,19},{19,3},{4,20},{20... | collective-permute-start | bytes 98312 | tf_op jit(solution)/shard_map/ppermute | solution.py:445
  14.3 5.7 %collective-permute-start.3 = (f32[120,128]{1,0:T(8,128)S(1)}, f32[120,128]{1,0:T(8,128)S(1)}, u32[]{:S(2)}, u32[]{:S(2)}) collective-permute-start(f32[120,128]{1,0:T(8,128)S(1)} %add.10), channel_id=1, source_target_pairs={{0,4},{1,5},{2,6},{3,7},{4,0},{5,1},{6,2},{7,3},{8,12},{9,13},{10,... | collective-permute-start | bytes 184328 | tf_op jit(solution)/shard_map/ppermute | solution.py:454

commit v3 on v2

--- a/solution.py
+++ b/solution.py
@@ -20,9 +20,12 @@
 UNIT = 0.5 * SPACING
 FEATS = 16
 SUB = 8
+IN_FLIGHT = 64
+WORK = 4500 * 10**6
 LANES = 128
 CHUNK = 256
-U_PACK, U_TRANS, U_COLL, U_FACE = 25, 16, 16, 32
+CHUNK_OUT = 128
+U_PACK, U_TRANS, U_COLL, U_FACE = 32, 32, 16, 16
 F32 = jnp.float32
 BF16 = jnp.bfloat16
 VMEM_LIMIT = 16 * 1024 * 1024
@@ -44,7 +47,9 @@
         group([pl.multiple_of((i * unroll + k) * SUB, SUB) for k in range(unroll)])
         return carry
 
-    if rounds:
+    if rounds == 1:
+        group([k * SUB for k in range(unroll)])
+    elif rounds:
         lax.fori_loop(0, rounds, step, 0)
     left = [k * SUB for k in range(rounds * unroll, whole)]
     if left:
@@ -108,7 +113,7 @@
     return jnp.dot(left, right, preferred_element_type=F32)
 
 
-def pre_kernel(count, rows, orient_hbm, tan_hbm, st_hbm, ysend, xsend, mom, tab, tan_v, orient_ref, feat, wide, edge, st_v, sems):
+def pre_kernel(count, rows, orient_hbm, tan_hbm, st_hbm, ysend, xsend, mom, tab, tan_v, orient_ref, total_v, feat, wide, edge, st_v, sems):
     comps = 3 * rows
     padded = feat.shape[1]
     starts = list(range(0, padded, CHUNK))
@@ -120,7 +125,7 @@
             copies.append(pltpu.make_async_copy(src.at[part], dst.at[part], sems.at[a * len(starts) + j]))
     signs = pltpu.make_async_copy(orient_hbm, orient_ref, sems.at[2 * len(starts)])
     signs.start()
-    for copy in copies:
+    for copy in copies[:IN_FLIGHT]:
         copy.start()
     tail = (padded - count) * comps
     for buf in (tan_v, st_v):
@@ -137,50 +142,52 @@
     scale = away.astype(F32)
     wide[...] = dot(flipped, spread_table([(13, 1.0), (14, 1.0)], 1))
     face = jnp.where(away == 1, rows - 1, 0)
-    sub = iota((SUB, LANES), 0)
-    low = sub % 4 < 2
+    low = iota((SUB, LANES), 0) % 4 < 2
     lane = iota((SUB, LANES), 1)
-    for copy in copies[: len(starts)]:
-        copy.wait()
-
-    def pack(start):
-        at = lambda comp, row: tan_v[pl.ds(start * comps + comp * rows + row, SUB, stride=comps), :]
-        sx = wide[pl.ds(start, SUB), 0:LANES]
-        sy = wide[pl.ds(start, SUB), LANES : 2 * LANES]
-        center, grad_x, grad_y = at(0, face), at(1, face), at(2, face)
-        out_y = center + sy * grad_y
-        own = jnp.where(low, out_y, grad_x)
-        other = jnp.where(low, grad_x, out_y)
-        packed = jnp.where(sy * scale > 0.0, own, swap_pairs(other, low))
-        right = sx > 0.0
-        acc = jnp.zeros((SUB, LANES), F32)
-        for row in range(rows):
-            slope = at(2, row)
-            value = at(0, row) + sx * at(1, row)
-            for j, piece in ((2 * row, value), (2 * row + 1, slope)):
-                here = jnp.where(right, pltpu.roll(piece, 1 + j, 1), pltpu.roll(piece, j, 1) if j else piece)
-                acc = jnp.where(lane == j, here, acc)
-        where = (pl.ds(start, SUB), slice(None))
-        return [(ysend, where, packed), (edge, where, acc)]
-
-    for_blocks(count, pack, U_PACK)
-    xsend[...] = edge[...].T[0 : xsend.shape[0], :]
     table = table.astype(BF16)
+    sums = [[total_v.at[pl.ds((a * comps + c) * FEATS, FEATS)] for c in range(comps)] for a in range(2)]
     for a, buf in enumerate((tan_v, st_v)):
-        if a:
-            for copy in copies[len(starts) :]:
-                copy.wait()
-        for c in range(comps):
-            total = jnp.zeros((FEATS, LANES), F32)
-            for start in starts:
-                size = min(CHUNK, padded - start)
+        for j, start in enumerate(starts):
+            copies[a * len(starts) + j].wait()
+            for copy in copies[a * len(starts) + j + IN_FLIGHT :][:1]:
+                copy.start()
+
+            def pack(local):
+                first = start + local
+                at = lambda comp, row: buf[pl.ds(first * comps + comp * rows + row, SUB, stride=comps), :]
+                where = (pl.ds(first, SUB), slice(None))
+                sx = wide[pl.ds(first, SUB), 0:LANES]
+                sy = wide[pl.ds(first, SUB), LANES : 2 * LANES]
+                center, grad_x, grad_y = at(0, face), at(1, face), at(2, face)
+                out_y = center + sy * grad_y
+                own = jnp.where(low, out_y, grad_x)
+                other = jnp.where(low, grad_x, out_y)
+                packed = jnp.where(sy * scale > 0.0, own, swap_pairs(other, low))
+                right = sx > 0.0
+                acc = jnp.zeros((SUB, LANES), F32)
+                for row in range(rows):
+                    slope = at(2, row)
+                    value = at(0, row) + sx * at(1, row)
+                    for j, piece in ((2 * row, value), (2 * row + 1, slope)):
+                        here = jnp.where(right, pltpu.roll(piece, 1 + j, 1), pltpu.roll(piece, j, 1) if j else piece)
+                        acc = jnp.where(lane == j, here, acc)
+                return [(ysend, where, packed), (edge, where, acc)]
+
+            if a == 0:
+                for_blocks(min(CHUNK, count - start), pack, U_PACK)
+            size = min(CHUNK, padded - start)
+            part = table[:, start : start + size]
+            for c in range(comps):
                 data = buf[pl.ds(start * comps + c, size, stride=comps), :]
                 high = data.astype(BF16)
                 rest = (data - high.astype(F32)).astype(BF16)
-                part = table[:, start : start + size]
-                total = total + dot(part, high) + dot(part, rest)
-            ones = total[0:1]
-            squares = 4.0 * total[4:7] + ones
+                new = dot(part, high) + dot(part, rest)
+                sums[a][c][...] = new if j == 0 else sums[a][c][...] + new
+        if a == 0:
+            xsend[...] = edge[...].T[0 : xsend.shape[0], :]
+        for c in range(comps):
+            total = sums[a][c][...]
+            squares = 4.0 * total[4:7] + total[0:1]
             cross = total[7:10] + total[10:13]
             slot = (1 - a) * comps + c
             mom[pl.ds(slot * 8, 4), :] = total[0:4]
@@ -319,7 +326,7 @@
     return [const] + [UNIT * l for l in linear] + [4.0 * s for s in square[:3]] + square[3:] + square[3:]
 
 
-def collide_kernel(count, rows, mom, tab, adv, out, raw, turn, coef, power):
+def collide_kernel(count, rows, mom, tab, adv, out_hbm, kept, raw, turn, coef, power, out, sems):
     comps = 3 * rows
     spots = 4 * rows
     weight = SPACING**3
@@ -369,9 +376,12 @@
             for j, piece in enumerate(pieces(turn[pl.ds(s, FEATS, stride=spots), :])):
                 coef[pl.ds(j * FEATS, FEATS), lanes] = piece
     root3 = 3.0 * GAUSS
-    for start in range(0, count, CHUNK):
-        size = min(CHUNK, count - start)
-        power[...] = dot(tab[pl.ds(start, CHUNK), :], coef[...])
+    face = jnp.where(towards() == 1, rows - 1, 0)
+    copies = []
+    for j, start in enumerate(range(0, count, CHUNK_OUT)):
+        size = min(CHUNK_OUT, count - start)
+        half_power = power.at[j % 2]
+        half_power[...] = dot(tab[pl.ds(start, CHUNK_OUT), :], coef[...])
 
         def block(local):
             first = (start + local) * comps
@@ -380,8 +390,8 @@
                 gd = []
                 for q in range(4):
                     lane = (q * rows + row) * LANES
-                    expo = power[pl.ds(local, SUB), lane : lane + LANES]
-                    factor = power[pl.ds(local, SUB), spots * LANES + lane : spots * LANES + lane + LANES]
+                    expo = half_power[pl.ds(local, SUB), lane : lane + LANES]
+                    factor = half_power[pl.ds(local, SUB), spots * LANES + lane : spots * LANES + lane + LANES]
                     gd.append(jnp.exp2(expo) * factor)
                 back, front = gd[0] + gd[1], gd[2] + gd[3]
                 collided = (back + front, root3 * (front - back), root3 * ((gd[1] - gd[0]) + (gd[3] - gd[2])))
@@ -391,20 +401,23 @@
             return stores
 
         for_blocks(size, block, U_COLL)
-
-
-def face_kernel(count, rows, col, tab, yrecv, out_hbm, out_v, wide, sems):
-    comps = 3 * rows
-    away = towards()
-    scale = away.astype(F32)
-    face = jnp.where(away == 1, rows - 1, 0)
+        part = pl.ds(start * comps, size * comps)
+        copies.append(pltpu.make_async_copy(out.at[part], out_hbm.at[part], sems.at[j]))
+        copies[-1].start()
+        part = pl.ds(start * 3, size * 3)
+        kept[part, :] = out[pl.ds(start * comps + face, size * 3, stride=rows), :]
+    for copy in copies:
+        copy.wait()
+
+
+def face_kernel(count, rows, kept, tab, yrecv, before, out, face_v, wide, sems):
+    scale = towards().astype(F32)
+    face = jnp.where(towards() == 1, rows - 1, 0)
     wide[...] = dot(tab[...], spread_table([(15, UNIT), (14, scale)], 1))
     low = iota((SUB, LANES), 0) % 4 < 2
     copies = []
-    for j, start in enumerate(range(0, count, CHUNK)):
-        size = min(CHUNK, count - start)
-        part = pl.ds(start * comps, size * comps)
-        out_v[part, :] = col[part, :]
+    for j, start in enumerate(range(0, count, CHUNK_OUT)):
+        size = min(CHUNK_OUT, count - start)
 
         def block(local):
             at = start + local
@@ -417,18 +430,19 @@
             slope = speed * jnp.where(low, turned, data)
             stores = []
             for comp, term in enumerate((value, slope, (3.0 * scale) * value)):
-                where = pl.ds(at * comps + comp * rows + face, SUB, stride=comps)
-                stores.append((out_v, (where, slice(None)), col[where, :] - term))
+                where = pl.ds(at * 3 + comp, SUB, stride=3)
+                stores.append((face_v, (where, slice(None)), kept[where, :] - term))
             return stores
 
         for_blocks(size, block, U_FACE)
-        copies.append(pltpu.make_async_copy(out_v.at[part], out_hbm.at[part], sems.at[j]))
+        part = pl.ds(start * 3, size * 3)
+        copies.append(pltpu.make_async_copy(face_v.at[part], out.at[part, face], sems.at[j]))
         copies[-1].start()
     for copy in copies:
         copy.wait()
 
 
-def call(kernel, out_shape, scratch, ins, outs, name):
+def call(kernel, out_shape, scratch, ins, outs, name, aliases={}, work=0):
     return pl.pallas_call(
         kernel,
         out_shape=out_shape,
@@ -436,6 +450,8 @@
         out_specs=jax.tree.map(lambda m: pl.BlockSpec(memory_space=m), outs),
         scratch_shapes=scratch,
         compiler_params=pltpu.CompilerParams(vmem_limit_bytes=VMEM_LIMIT),
+        input_output_aliases=aliases,
+        cost_estimate=pl.CostEstimate(flops=work, transcendentals=0, bytes_accessed=0) if work else None,
         name=name,
     )
 
@@ -445,15 +461,13 @@
     return lax.ppermute(value, axis, [(i, (i + by) % devices) for i in range(devices)])
 
 
-def sum_over(value, axis, beside):
+def sum_over(value, axis):
     devices = lax.axis_size(axis)
     step = 1
     while step < devices:
-        if step == 4:
-            value, *beside = lax.optimization_barrier((value, *beside))
         value = value + lax.ppermute(value, axis, [(i, i ^ step) for i in range(devices)])
         step *= 2
-    return value, beside
+    return value
 
 
 def shards(state, tangent, orient, walls):
@@ -479,6 +493,7 @@
         ),
         [
             pltpu.VMEM((2, count), jnp.int32),
+            pltpu.VMEM((2 * comps * FEATS, cols), F32),
             pltpu.VMEM((FEATS, padded), F32),
             pltpu.VMEM((padded, 2 * LANES), F32),
             pltpu.VMEM((padded, LANES), F32),
@@ -492,8 +507,8 @@
     yrecv = lax.ppermute(ysend, "gy", [(0, 1), (1, 0)])
     single = lax.axis_size("gx") == 2
     edges = (exchange(xsend, "gx", 1),) + (() if single else (exchange(xsend, "gx", -1),))
-    mom, edges = sum_over(mom, "vert", edges)
-    edges += [] if single else [signs]
+    mom = sum_over(mom, "vert")
+    edges += () if single else (signs,)
     adv = call(
         functools.partial(transport_kernel, count, rows, cols, single),
         shape((total_rows, cols), F32),
@@ -501,32 +516,36 @@
         (vm,) * (3 + len(edges)),
         vm,
         "transport",
+        work=WORK,
     )(tan_v, tab, walls, *edges)
-    col = call(
+    col, kept = call(
         functools.partial(collide_kernel, count, rows),
-        shape((total_rows, cols), F32),
+        (shape((total_rows, cols), F32), shape((count * 3, cols), F32)),
         [
             pltpu.VMEM((4 * rows * 24, LANES), F32),
             pltpu.VMEM((FEATS * 4 * rows, LANES), F32),
             pltpu.VMEM((LANES, 8 * rows * LANES), BF16),
-            pltpu.VMEM((CHUNK, 8 * rows * LANES), F32),
+            pltpu.VMEM((2, CHUNK_OUT, 8 * rows * LANES), F32),
+            pltpu.VMEM((total_rows, cols), F32),
+            pltpu.SemaphoreType.DMA((padded // CHUNK_OUT,)),
         ],
         (vm, vm, vm),
-        vm,
+        (hbm, vm),
         "collide",
     )(mom, tab, adv)
     out = call(
         functools.partial(face_kernel, count, rows),
-        shape((total_rows, cols), F32),
+        shape((count * 3, rows, cols), F32),
         [
-            pltpu.VMEM((total_rows, cols), F32),
+            pltpu.VMEM((count * 3, cols), F32),
             pltpu.VMEM((padded, 2 * LANES), F32),
-            pltpu.SemaphoreType.DMA((chunks,)),
+            pltpu.SemaphoreType.DMA((padded // CHUNK_OUT,)),
         ],
-        (vm, vm, vm),
+        (vm, vm, vm, hbm),
         hbm,
         "faces",
-    )(col, tab, yrecv)
+        {3: 0},
+    )(kept, tab, yrecv, col.reshape(count * 3, rows, cols))
     return out.reshape(state.shape)
 
 

time: 24.7 us -> 20.6 us (0.83)
  waiting for transfers between devices: 4.1 us -> 1.29 us
  Pallas kernels: 11.6 us -> 10.2 us
    ppermute x3, waiting for transfers between devices: 2.84 us -> 1.18 us  [sum_over(): lax.ppermute(value, axis, [(i, i ^ step) for i in range(devices)])]
    ppermute x1, waiting for transfers between devices: 1.26 us -> 0.01 us  [exchange(): lax.ppermute(value, axis, [(i, (i + by) % devices) for i in range(devices)])]
    pallas_call x1, Pallas kernels: 4.46 us -> 3.73 us  [shards(): call(functools.partial(pre_kernel, count, rows), (shape((count, cols), F3...]
    ppermute x3, starting transfers between devices: 4.23 us -> 4.81 us  [sum_over(): lax.ppermute(value, axis, [(i, i ^ step) for i in range(devices)])]
    pallas_call x2, Pallas kernels: 4.56 us -> 4 us  [the longest x1 2.62 us: shards(): call(functools.partial(collide_kernel, count, rows), (shape((total_rows,...]
    ppermute x1, starting transfers between devices: 2.97 us -> 2.56 us  [shards(): yrecv = lax.ppermute(ysend, 'gy', [(0, 1), (1, 0)])]
  transfers between devices with their start and end apart: 5 -> 5, of which waited for: 4 -> 3; matrix products, arithmetic and copies ran while one was open for 0% -> 0% of each run, Pallas kernels for 21% -> 25%
where the time goes in v3:
time: 20.6 us; the launch traced here: 20.4 us
  Pallas kernels  10.2 us (50%)
  starting transfers between devices  8.89 us (43%)
  waiting for transfers between devices  1.29 us (6%)
    ppermute x3, starting transfers between devices, sum_over(): lax.ppermute(value, axis, [(i, i ^ step) for i in range(devices)])  4.81 us
    pallas_call x1, Pallas kernels, shards(): call(functools.partial(pre_kernel, count, rows), (shape((count, cols), F3...  3.73 us
    pallas_call x1, Pallas kernels, shards(): call(functools.partial(collide_kernel, count, rows), (shape((total_rows,...  2.62 us
    ppermute x1, starting transfers between devices, shards(): yrecv = lax.ppermute(ysend, 'gy', [(0, 1), (1, 0)])  2.56 us
    pallas_call x1, Pallas kernels, shards(): call(functools.partial(transport_kernel, count, rows, cols, single), shap...  2.48 us
    ppermute x1, starting transfers between devices, exchange(): lax.ppermute(value, axis, [(i, (i + by) % devices) for i in range(devices)])  1.52 us
    pallas_call x1, Pallas kernels, shards(): call(functools.partial(face_kernel, count, rows), shape((count * 3, rows,...  1.37 us
    ppermute x3, waiting for transfers between devices, sum_over(): lax.ppermute(value, axis, [(i, i ^ step) for i in range(devices)])  1.18 us
  transfers between devices with their start and end apart: 5, of which 3 were waited for; matrix products, arithmetic and copies ran while one was open for 0% of the time, Pallas kernels for 25%

profile of v3, /device:TPU:0, one launch (start us, length us, event | category | flops | bytes accessed | tf_op | source)
XLA Modules:
  0.0 20.4 jit_solution(2114460498252084791)
XLA Ops:
  0.0 0.0 copy-start
  0.0 3.7 %pack_and_moments.1 = (f32[1000,128]{1,0:T(8,128)S(1)}, f32[8,1024]{1,0:T(8,128)S(1)}, f32[120,128]{1,0:T(8,128)S(1)}, bf16[1024,128]{1,0:T(8,128)(2,1)S(1)}, f32[6144,128]{1,0:T(8,128)S(1)}) custom-call(s32[2,1000]{1,0:T(2,128)} %bitcast.8, f32[6000,128]{1,0:T(8,128)} %bitcast.5, f32[6000,128]{1,0:T(8,128)} %bitcast.6), custom_call_target="tpu_custom_call" | custom-call | tf_op jit(solution)/shard_map/pack_and_moments/pallas_call | solution.py:485
  3.7 0.5 %collective-permute-start = (f32[120,128]{1,0:T(8,128)S(1)}, f32[120,128]{1,0:T(8,128)S(1)}, u32[]{:S(2)}, u32[]{:S(2)}) collective-permute-start(f32[120,128]{1,0:T(8,128)S(1)} %get-tuple-element.12), channel_id=1, source_target_pairs={{0,1},{1,0},{2,3},{3,2},{4,5},{5,4},{6,7},{7,6},{8,9},{9,8},{10,11... | collective-permute-start | bytes 184328 | tf_op jit(solution)/shard_map/ppermute | solution.py:468
  4.3 2.6 %collective-permute-start.4 = (f32[1000,128]{1,0:T(8,128)S(1)}, f32[1000,128]{1,0:T(8,128)S(1)}, u32[]{:S(2)}, u32[]{:S(2)}) collective-permute-start(f32[1000,128]{1,0:T(8,128)S(1)} %get-tuple-element.17), channel_id=1, source_target_pairs={{0,8},{8,0},{1,9},{9,1},{2,10},{10,2},{3,11},{11,3},{4,12},{12,4},... | collective-permute-start | bytes 1536008 | tf_op jit(solution)/shard_map/ppermute | solution.py:507
  6.8 0.0 collective-permute-done
  6.8 1.6 %collective-permute-start.1 = (f32[120,128]{1,0:T(8,128)S(1)}, f32[120,128]{1,0:T(8,128)S(1)}, u32[]{:S(2)}, u32[]{:S(2)}) collective-permute-start(f32[120,128]{1,0:T(8,128)S(1)} %add.9), channel_id=1, source_target_pairs={{0,2},{1,3},{2,0},{3,1},{4,6},{5,7},{6,4},{7,5},{8,10},{9,11},{10,... | collective-permute-start | bytes 184328 | tf_op jit(solution)/shard_map/ppermute | solution.py:468
  8.5 1.5 %collective-permute-start.3 = (f32[8,1024]{1,0:T(8,128)S(1)}, f32[8,1024]{1,0:T(8,128)S(1)}, u32[]{:S(2)}, u32[]{:S(2)}) collective-permute-start(f32[8,1024]{1,0:T(8,128)S(1)} %get-tuple-element.15), channel_id=1, source_target_pairs={{0,16},{16,0},{1,17},{17,1},{2,18},{18,2},{3,19},{19,3},{4,20},{20... | collective-permute-start | bytes 98312 | tf_op jit(solution)/shard_map/ppermute | solution.py:461
  10.0 1.1 %collective-permute-done.1 = f32[120,128]{1,0:T(8,128)S(1)} collective-permute-done((f32[120,128]{1,0:T(8,128)S(1)}, f32[120,128]{1,0:T(8,128)S(1)}, u32[]{:S(2)}, u32[]{:S(2)}) %collective-permute-start.1) | collective-permute-done | bytes 61472 | tf_op jit(solution)/shard_map/ppermute | solution.py:468
  11.1 2.7 %collective-permute-start.2 = (f32[120,128]{1,0:T(8,128)S(1)}, f32[120,128]{1,0:T(8,128)S(1)}, u32[]{:S(2)}, u32[]{:S(2)}) collective-permute-start(f32[120,128]{1,0:T(8,128)S(1)} %add.10), channel_id=1, source_target_pairs={{0,4},{1,5},{2,6},{3,7},{4,0},{5,1},{6,2},{7,3},{8,12},{9,13},{10,... | collective-permute-start | bytes 184328 | tf_op jit(solution)/shard_map/ppermute | solution.py:468
  13.8 0.0 collective-permute-done.3.refs_3_
  13.8 0.0 copy-done
  13.8 2.5 %transport.1.adv = f32[6000,128]{1,0:T(8,128)S(1)} custom-call(f32[6144,128]{1,0:T(8,128)S(1)} %get-tuple-element.14.refs_0_, bf16[1024,128]{1,0:T(8,128)(2,1)S(1)} %get-tuple-element.13.refs_1_.tab, s32[2,128]{1,0:T(2,128)S(1)} %copy-done, f32[8,1024]{1,0:T(8,128)S(1)} %collective-permute-done.3.refs_3_), custom_call_target="tpu_custom_call" | custom-call | flops 4499999744 | tf_op jit(solution)/shard_map/transport/pallas_call | solution.py:512
  16.3 0.1 collective-permute-done.2
  16.3 2.6 %collide.1 = (f32[6000,128]{1,0:T(8,128)}, f32[3000,128]{1,0:T(8,128)S(1)}) custom-call(f32[120,128]{1,0:T(8,128)S(1)} %add.11.mom, bf16[1024,128]{1,0:T(8,128)(2,1)S(1)} %get-tuple-element.13.refs_1_.tab, f32[6000,128]{1,0:T(8,128)S(1)} %transport.1.adv), custom_call_target="tpu_custom_call" | custom-call | tf_op jit(solution)/shard_map/collide/pallas_call | solution.py:521
  19.0 0.1 collective-permute-done.4.yrecv
  19.1 1.4 %faces.1 = f32[3000,2,128]{2,1,0:T(2,128)} custom-call(f32[3000,128]{1,0:T(8,128)S(1)} %get-tuple-element.16.kept, bf16[1024,128]{1,0:T(8,128)(2,1)S(1)} %get-tuple-element.13.refs_1_.tab, f32[1000,128]{1,0:T(8,128)S(1)} %collective-permute-done.4.yrecv, f32[3000,2,128]{2,1,0:T(2,128)} %bitcast.7), custom_call_target="tpu_custom_call", output_to_operand_aliasing={{}: (3, {})} | custom-call | tf_op jit(solution)/shard_map/faces/pallas_call | solution.py:536
  (3 shorter events, 0.0 us)
Async XLA Ops:
  0.0 13.8 %copy-start = (s32[2,128]{1,0:T(2,128)S(1)}, s32[2,128]{1,0:T(2,128)}, u32[]{:S(2)}) copy-start(s32[2,128]{1,0:T(2,128)} %refs_2_.1) | copy-start | bytes 3076
  3.7 3.1 %collective-permute-start = (f32[120,128]{1,0:T(8,128)S(1)}, f32[120,128]{1,0:T(8,128)S(1)}, u32[]{:S(2)}, u32[]{:S(2)}) collective-permute-start(f32[120,128]{1,0:T(8,128)S(1)} %get-tuple-element.12), channel_id=1, source_target_pairs={{0,1},{1,0},{2,3},{3,2},{4,5},{5,4},{6,7},{7,6},{8,9},{9,8},{10,11... | collective-permute-start | bytes 184328 | tf_op jit(solution)/shard_map/ppermute | solution.py:468
  4.3 14.8 %collective-permute-start.4 = (f32[1000,128]{1,0:T(8,128)S(1)}, f32[1000,128]{1,0:T(8,128)S(1)}, u32[]{:S(2)}, u32[]{:S(2)}) collective-permute-start(f32[1000,128]{1,0:T(8,128)S(1)} %get-tuple-element.17), channel_id=1, source_target_pairs={{0,8},{8,0},{1,9},{9,1},{2,10},{10,2},{3,11},{11,3},{4,12},{12,4},... | collective-permute-start | bytes 1536008 | tf_op jit(solution)/shard_map/ppermute | solution.py:507
  6.8 4.3 %collective-permute-start.1 = (f32[120,128]{1,0:T(8,128)S(1)}, f32[120,128]{1,0:T(8,128)S(1)}, u32[]{:S(2)}, u32[]{:S(2)}) collective-permute-start(f32[120,128]{1,0:T(8,128)S(1)} %add.9), channel_id=1, source_target_pairs={{0,2},{1,3},{2,0},{3,1},{4,6},{5,7},{6,4},{7,5},{8,10},{9,11},{10,... | collective-permute-start | bytes 184328 | tf_op jit(solution)/shard_map/ppermute | solution.py:468
  8.5 5.3 %collective-permute-start.3 = (f32[8,1024]{1,0:T(8,128)S(1)}, f32[8,1024]{1,0:T(8,128)S(1)}, u32[]{:S(2)}, u32[]{:S(2)}) collective-permute-start(f32[8,1024]{1,0:T(8,128)S(1)} %get-tuple-element.15), channel_id=1, source_target_pairs={{0,16},{16,0},{1,17},{17,1},{2,18},{18,2},{3,19},{19,3},{4,20},{20... | collective-permute-start | bytes 98312 | tf_op jit(solution)/shard_map/ppermute | solution.py:461
  11.1 5.2 %collective-permute-start.2 = (f32[120,128]{1,0:T(8,128)S(1)}, f32[120,128]{1,0:T(8,128)S(1)}, u32[]{:S(2)}, u32[]{:S(2)}) collective-permute-start(f32[120,128]{1,0:T(8,128)S(1)} %add.10), channel_id=1, source_target_pairs={{0,4},{1,5},{2,6},{3,7},{4,0},{5,1},{6,2},{7,3},{8,12},{9,13},{10,... | collective-permute-start | bytes 184328 | tf_op jit(solution)/shard_map/ppermute | solution.py:468

commit v4 on v3

--- a/solution.py
+++ b/solution.py
@@ -25,7 +25,7 @@
 LANES = 128
 CHUNK = 256
 CHUNK_OUT = 128
-U_PACK, U_TRANS, U_COLL, U_FACE = 32, 32, 16, 16
+U_PACK, U_EDGE, U_TRANS, U_COLL, U_FACE = 32, 31, 16, 16, 16
 F32 = jnp.float32
 BF16 = jnp.bfloat16
 VMEM_LIMIT = 16 * 1024 * 1024
@@ -58,8 +58,8 @@
         group([count - SUB])
 
 
-def swap_pairs(value, low):
-    return jnp.where(low, pltpu.roll(value, SUB - 2, 0), pltpu.roll(value, 2, 0))
+def swap_rows(value, first, by):
+    return jnp.where(first, pltpu.roll(value, SUB - by, 0), pltpu.roll(value, by, 0))
 
 
 def iota(shape, dim):
@@ -92,7 +92,7 @@
         feat[k : k + 1, 0:count] = row
 
 
-def spread_table(columns, step):
+def spread_table(columns):
     rows = iota((LANES, LANES * len(columns)), 0)
     blocks = iota((LANES, LANES * len(columns)), 1) // LANES
     out = jnp.zeros(rows.shape, F32)
@@ -113,7 +113,7 @@
     return jnp.dot(left, right, preferred_element_type=F32)
 
 
-def pre_kernel(count, rows, orient_hbm, tan_hbm, st_hbm, ysend, xsend, mom, tab, tan_v, orient_ref, total_v, feat, wide, edge, st_v, sems):
+def pre_kernel(count, rows, orient_hbm, tan_hbm, st_hbm, ysend, mom, tab, tan_v, wide, orient_ref, total_v, feat, st_v, sems):
     comps = 3 * rows
     padded = feat.shape[1]
     starts = list(range(0, padded, CHUNK))
@@ -131,7 +131,6 @@
     for buf in (tan_v, st_v):
         if tail:
             buf[pl.ds(count * comps, tail), :] = jnp.zeros((tail, LANES), F32)
-    edge[...] = jnp.zeros(edge.shape, F32)
     signs.wait()
     fill_features(feat, orient_ref, count)
     table = feat[...]
@@ -140,10 +139,10 @@
     tab[...] = flipped
     away = towards()
     scale = away.astype(F32)
-    wide[...] = dot(flipped, spread_table([(13, 1.0), (14, 1.0)], 1))
+    for j, column in enumerate(((1, UNIT), (15, UNIT), (13, 1.0), (14, scale))):
+        wide[pl.ds(j * padded, padded), :] = dot(flipped, spread_table([column]))
     face = jnp.where(away == 1, rows - 1, 0)
     low = iota((SUB, LANES), 0) % 4 < 2
-    lane = iota((SUB, LANES), 1)
     table = table.astype(BF16)
     sums = [[total_v.at[pl.ds((a * comps + c) * FEATS, FEATS)] for c in range(comps)] for a in range(2)]
     for a, buf in enumerate((tan_v, st_v)):
@@ -155,23 +154,13 @@
             def pack(local):
                 first = start + local
                 at = lambda comp, row: buf[pl.ds(first * comps + comp * rows + row, SUB, stride=comps), :]
-                where = (pl.ds(first, SUB), slice(None))
-                sx = wide[pl.ds(first, SUB), 0:LANES]
-                sy = wide[pl.ds(first, SUB), LANES : 2 * LANES]
+                toward = wide[pl.ds(3 * padded + first, SUB), :]
                 center, grad_x, grad_y = at(0, face), at(1, face), at(2, face)
-                out_y = center + sy * grad_y
+                out_y = center + (toward * scale) * grad_y
                 own = jnp.where(low, out_y, grad_x)
                 other = jnp.where(low, grad_x, out_y)
-                packed = jnp.where(sy * scale > 0.0, own, swap_pairs(other, low))
-                right = sx > 0.0
-                acc = jnp.zeros((SUB, LANES), F32)
-                for row in range(rows):
-                    slope = at(2, row)
-                    value = at(0, row) + sx * at(1, row)
-                    for j, piece in ((2 * row, value), (2 * row + 1, slope)):
-                        here = jnp.where(right, pltpu.roll(piece, 1 + j, 1), pltpu.roll(piece, j, 1) if j else piece)
-                        acc = jnp.where(lane == j, here, acc)
-                return [(ysend, where, packed), (edge, where, acc)]
+                packed = jnp.where(toward > 0.0, own, swap_rows(other, low, 2))
+                return [(ysend, (pl.ds(first, SUB), slice(None)), packed)]
 
             if a == 0:
                 for_blocks(min(CHUNK, count - start), pack, U_PACK)
@@ -183,8 +172,6 @@
                 rest = (data - high.astype(F32)).astype(BF16)
                 new = dot(part, high) + dot(part, rest)
                 sums[a][c][...] = new if j == 0 else sums[a][c][...] + new
-        if a == 0:
-            xsend[...] = edge[...].T[0 : xsend.shape[0], :]
         for c in range(comps):
             total = sums[a][c][...]
             squares = 4.0 * total[4:7] + total[0:1]
@@ -196,81 +183,129 @@
             mom[pl.ds(2 * comps * 8 + slot * 2, 2), :] = cross[1:3]
 
 
+def pair_reader(tan_v, comps, rows, start):
+    return lambda comp, row, odd: tan_v[
+        pl.ds((2 * start + odd) * comps + comp * rows + row, SUB, stride=2 * comps), :
+    ]
+
+
+def edge_kernel(count, rows, tan_v, wide, xsend, edge):
+    comps = 3 * rows
+    lane = iota((SUB, LANES), 1)
+    last = lane == LANES - 1
+    inside = jnp.logical_not(last | (lane == 0))
+    sign = jnp.where(last, 1.0, -1.0)
+    tail = edge.shape[0] - count // 2
+    if tail:
+        edge[pl.ds(count // 2, tail), :] = jnp.zeros((tail, LANES), F32)
+
+    def block(start):
+        at = pair_reader(tan_v, comps, rows, start)
+        even = wide[pl.ds(4 * edge.shape[0] + 2 * start, SUB, stride=2), :] * sign > 0.0
+        held = []
+        for row in range(rows):
+            center, grad_x, grad_y = (jnp.where(even, at(c, row, 0), at(c, row, 1)) for c in range(3))
+            held.append(jnp.where(inside, 0.0, center + sign * grad_x))
+            held.append(jnp.where(inside, 0.0, grad_y))
+        shift = 2
+        while len(held) > 1:
+            pairs = zip(held[0::2], held[1::2])
+            held = [p + pltpu.roll(q, shift, 1) for p, q in pairs] + held[len(held) // 2 * 2 :]
+            shift *= 2
+        return [(edge, (pl.ds(start, SUB), slice(None)), held[0])]
+
+    for_blocks(count // 2, block, U_EDGE)
+    turned = edge[...].T
+    size = xsend.shape[0]
+    xsend[...] = jnp.concatenate([turned[0 : size - 1], turned[LANES - 1 : LANES]], axis=0)
+
+
 def transport_kernel(count, rows, cols, single, *refs):
-    tan_v, tab, walls, behind = refs[:4]
-    adv, wide = refs[-2:]
+    tan_v, wide, walls, behind = refs[:4]
+    adv, ends = refs[-2:]
     comps = 3 * rows
-    padded = tab.shape[0]
+    pairs = ends.shape[0]
     away = towards()
     scale = away.astype(F32)
     arrived = behind[...]
     if not single:
-        ahead, signs = refs[4:6]
-        spare = [jnp.zeros((1, padded - count), jnp.int32)] if padded > count else []
-        right_row = jnp.concatenate([signs[0:1, :]] + spare, axis=1) == 1
-        arrived = jnp.where(right_row, arrived, ahead[...])
-    spare = jnp.zeros((LANES - 3 * SUB, padded), F32)
+        arrived = jnp.where(iota((SUB, pairs), 0) % 2 == 1, arrived, refs[4][...])
+    spare = jnp.zeros((LANES - 3 * SUB, pairs), F32)
     parts = [piece.astype(F32) for piece in pieces(arrived)]
-    edges = jnp.concatenate(parts + [spare], axis=0).T.astype(BF16)
-    cols_w = [(1, UNIT), (2, UNIT), (15, UNIT), (13, 1.0), (14, scale)]
-    wide[:, 0 : 5 * LANES] = dot(tab[...], spread_table(cols_w, 1))
-    r = iota((LANES, LANES * 2 * rows), 0)
-    b = iota((LANES, LANES * 2 * rows), 1) // LANES
-    pick = jnp.where((r % SUB == b) & (r < 3 * SUB), 1.0, 0.0).astype(BF16)
-    wide[:, 5 * LANES : (5 + 2 * rows) * LANES] = dot(edges, pick)
-    sub = iota((SUB, LANES), 0)
-    low = sub % 4 < 2
+    received = jnp.concatenate(parts + [spare], axis=0).T.astype(BF16)
+    r = iota((LANES, ends.shape[1]), 0)
+    b = iota((LANES, ends.shape[1]), 1) // LANES
+    row_of = jnp.where(b < 2 * rows, (2 * b + SUB - 1) % SUB, 2 * (b - 2 * rows))
+    pick = jnp.where((r % SUB == row_of) & (r < 3 * SUB), 1.0, 0.0).astype(BF16)
+    ends[...] = dot(received, pick)
+    first = iota((SUB, LANES), 0) % 2 == 0
     lane = iota((SUB, LANES), 1)
-    ends = jnp.where(lane == cols - 1, 1.0, 0.0) - jnp.where(lane == 0, 1.0, 0.0)
     wall_row = jnp.where(away == 1, walls[0:1, :], walls[1:2, :]).astype(F32)
     wall = jnp.broadcast_to(wall_row, (SUB, LANES))
     order = [jnp.where(away == 1, k, rows - 1 - k) for k in range(rows)]
 
     def block(start):
-        at = lambda comp, row: tan_v[pl.ds(start * comps + comp * rows + row, SUB, stride=comps), :]
-        col = lambda j: wide[pl.ds(start, SUB), j * LANES : (j + 1) * LANES]
-        vx, vy, ay, sx, toward_sign = (col(j) for j in range(5))
+        at = pair_reader(tan_v, comps, rows, start)
+        col = lambda j: wide[pl.ds(2 * (j * pairs + start), SUB, stride=2), :]
+        vx, ay, sx, toward_sign = (col(j) for j in range(4))
         ax = vx * sx
         sy = toward_sign * scale
-        right = sx > 0.0
+        vy3 = 3.0 * (ay * sy)
+        even = sx > 0.0
         toward = toward_sign > 0.0
-        outgoing = sx * ends > 0.0
-        center = [at(0, order[k]) for k in range(rows)]
-        grad_x = [at(1, order[k]) for k in range(rows)]
-        grad_y = [at(2, order[k]) for k in range(rows)]
-        out_y = [c + sy * g for c, g in zip(center, grad_y)]
+        loaded = [[(at(c, order[k], 0), at(c, order[k], 1)) for c in range(3)] for k in range(rows)]
+        results = []
+        for side in range(2):
+            take = (lambda e, o: jnp.where(even, e, o)) if side == 0 else (lambda e, o: jnp.where(even, o, e))
+            center, grad_x, grad_y = ([take(*loaded[k][c]) for k in range(rows)] for c in range(3))
+            out_y = [c + sy * g for c, g in zip(center, grad_y)]
+            edge_lane = lane == (0 if side == 0 else cols - 1)
+            vx3 = 3.0 * ax if side == 0 else -3.0 * ax
+            for k in range(rows):
+                column = (side * 2 * rows + 2 * order[k]) * LANES
+                edge = lambda j: ends[pl.ds(start, SUB), pl.ds(pl.multiple_of(column + j * LANES, LANES), LANES)]
+                inflow = lambda piece, j: jnp.where(edge_lane, edge(j), pltpu.roll(piece, 1 if side == 0 else cols - 1, 1))
+                out_x = center[k] + grad_x[k] if side == 0 else center[k] - grad_x[k]
+                in_x = inflow(out_x, 0)
+                in_xs = inflow(grad_y[k], 1)
+                if k == 0:
+                    near_v = wall * swap_rows(out_y[0], first, 1)
+                    near_s = wall * swap_rows(grad_x[0], first, 1)
+                else:
+                    near_v, near_s = out_y[k - 1], grad_x[k - 1]
+                if k == rows - 1:
+                    far_v, far_s = jnp.zeros_like(near_v), jnp.zeros_like(near_s)
+                else:
+                    far_v, far_s = out_y[k + 1], grad_x[k + 1]
+                in_y = jnp.where(toward, near_v, far_v)
+                in_ys = jnp.where(toward, near_s, far_s)
+                twice = 2.0 * center[k]
+                results.append(
+                    (
+                        ax * (out_x - in_x) + ay * (out_y[k] - in_y) + twice,
+                        vx3 * (out_x + in_x - twice) + ay * (grad_x[k] - in_ys) + 2.0 * grad_x[k],
+                        ax * (grad_y[k] - in_xs) + vy3 * (out_y[k] + in_y - twice) + 2.0 * grad_y[k],
+                    )
+                )
         stores = []
         for k in range(rows):
-            ecol = lambda j: wide[pl.ds(start, SUB), pl.ds(pl.multiple_of((5 + 2 * order[k] + j) * LANES, LANES), LANES)]
-            out_x = center[k] + sx * grad_x[k]
-
-            def inflow(piece, received):
-                mixed = jnp.where(outgoing, received, piece)
-                return jnp.where(right, pltpu.roll(mixed, 1, 1), pltpu.roll(mixed, cols - 1, 1))
-
-            in_x = inflow(out_x, ecol(0))
-            in_xs = inflow(grad_y[k], ecol(1))
-            if k == 0:
-                near_v = wall * swap_pairs(out_y[0], low)
-                near_s = wall * swap_pairs(grad_x[0], low)
-            else:
-                near_v, near_s = out_y[k - 1], grad_x[k - 1]
-            if k == rows - 1:
-                far_v, far_s = jnp.zeros_like(near_v), jnp.zeros_like(near_s)
-            else:
-                far_v, far_s = out_y[k + 1], grad_x[k + 1]
-            in_y = jnp.where(toward, near_v, far_v)
-            in_ys = jnp.where(toward, near_s, far_s)
-            twice = 2.0 * center[k]
-            mean = ax * (out_x - in_x) + ay * (out_y[k] - in_y) + twice
-            rate_x = 3.0 * vx * (out_x + in_x - twice) + ay * (grad_x[k] - in_ys) + 2.0 * grad_x[k]
-            rate_y = ax * (grad_y[k] - in_xs) + 3.0 * vy * (out_y[k] + in_y - twice) + 2.0 * grad_y[k]
-            for comp, value in enumerate((mean, rate_x, rate_y)):
-                where = pl.ds(start * comps + comp * rows + order[k], SUB, stride=comps)
-                stores.append((adv, (where, slice(None)), value))
+            for comp in range(3):
+                right, left = results[k][comp], results[rows + k][comp]
+                for odd in range(2):
+                    value = jnp.where(even, left, right) if odd else jnp.where(even, right, left)
+                    where = pl.ds((2 * start + odd) * comps + comp * rows + order[k], SUB, stride=2 * comps)
+                    stores.append((adv, (where, slice(None)), value))
         return stores
 
-    for_blocks(count, block, U_TRANS)
+    for_blocks(count // 2, block, U_TRANS)
+
+
+def face_terms(yrecv, at, speed, low):
+    data = yrecv[pl.ds(at, SUB), :]
+    turned = swap_rows(data, low, 2)
+    value = speed * jnp.where(low, data, turned)
+    slope = speed * jnp.where(low, turned, data)
+    return value, slope, (3.0 * towards().astype(F32)) * value
 
 
 def sym(entries):
@@ -410,10 +445,9 @@
         copy.wait()
 
 
-def face_kernel(count, rows, kept, tab, yrecv, before, out, face_v, wide, sems):
-    scale = towards().astype(F32)
+def face_kernel(count, rows, kept, wide, yrecv, before, out, face_v, sems):
     face = jnp.where(towards() == 1, rows - 1, 0)
-    wide[...] = dot(tab[...], spread_table([(15, UNIT), (14, scale)], 1))
+    padded = wide.shape[0] // 4
     low = iota((SUB, LANES), 0) % 4 < 2
     copies = []
     for j, start in enumerate(range(0, count, CHUNK_OUT)):
@@ -421,15 +455,10 @@
 
         def block(local):
             at = start + local
-            data = yrecv[pl.ds(at, SUB), :]
-            turned = swap_pairs(data, low)
-            speed = wide[pl.ds(at, SUB), 0:LANES]
-            sign = wide[pl.ds(at, SUB), LANES : 2 * LANES]
-            speed = jnp.where(sign < 0.0, speed, 0.0)
-            value = speed * jnp.where(low, data, turned)
-            slope = speed * jnp.where(low, turned, data)
+            ay, toward = (wide[pl.ds(j * padded + at, SUB), :] for j in (1, 3))
+            speed = jnp.where(toward > 0.0, 0.0, ay)
             stores = []
-            for comp, term in enumerate((value, slope, (3.0 * scale) * value)):
+            for comp, term in enumerate(face_terms(yrecv, at, speed, low)):
                 where = pl.ds(at * 3 + comp, SUB, stride=3)
                 stores.append((face_v, (where, slice(None)), kept[where, :] - term))
             return stores
@@ -482,21 +511,19 @@
     hold = [pltpu.with_memory_space_constraint(v, pltpu.HBM) for v in (signs, tn, st)]
     vm, hbm = pltpu.VMEM, pltpu.HBM
     shape = jax.ShapeDtypeStruct
-    ysend, xsend, mom, tab, tan_v = call(
+    ysend, mom, tab, tan_v, wide = call(
         functools.partial(pre_kernel, count, rows),
         (
             shape((count, cols), F32),
-            shape((SUB, padded), F32),
             shape((2 * comps * 10, cols), F32),
             shape((padded, LANES), BF16),
             shape((padded * comps, cols), F32),
+            shape((4 * padded, LANES), F32),
         ),
         [
             pltpu.VMEM((2, count), jnp.int32),
             pltpu.VMEM((2 * comps * FEATS, cols), F32),
             pltpu.VMEM((FEATS, padded), F32),
-            pltpu.VMEM((padded, 2 * LANES), F32),
-            pltpu.VMEM((padded, LANES), F32),
             pltpu.VMEM((padded * comps, cols), F32),
             pltpu.SemaphoreType.DMA((2 * chunks + 1,)),
         ],
@@ -505,19 +532,26 @@
         "pack_and_moments",
     )(*hold)
     yrecv = lax.ppermute(ysend, "gy", [(0, 1), (1, 0)])
+    xsend = call(
+        functools.partial(edge_kernel, count, rows),
+        shape((SUB, padded // 2), F32),
+        [pltpu.VMEM((padded // 2, LANES), F32)],
+        (vm, vm),
+        vm,
+        "edges",
+    )(tan_v, wide)
     single = lax.axis_size("gx") == 2
     edges = (exchange(xsend, "gx", 1),) + (() if single else (exchange(xsend, "gx", -1),))
     mom = sum_over(mom, "vert")
-    edges += () if single else (signs,)
     adv = call(
         functools.partial(transport_kernel, count, rows, cols, single),
         shape((total_rows, cols), F32),
-        [pltpu.VMEM((padded, (5 + 2 * rows) * LANES), F32)],
+        [pltpu.VMEM((padded // 2, 4 * rows * LANES), F32)],
         (vm,) * (3 + len(edges)),
         vm,
         "transport",
         work=WORK,
-    )(tan_v, tab, walls, *edges)
+    )(tan_v, wide, walls, *edges)
     col, kept = call(
         functools.partial(collide_kernel, count, rows),
         (shape((total_rows, cols), F32), shape((count * 3, cols), F32)),
@@ -529,7 +563,7 @@
             pltpu.VMEM((total_rows, cols), F32),
             pltpu.SemaphoreType.DMA((padded // CHUNK_OUT,)),
         ],
-        (vm, vm, vm),
+        (vm,) * 3,
         (hbm, vm),
         "collide",
     )(mom, tab, adv)
@@ -538,14 +572,13 @@
         shape((count * 3, rows, cols), F32),
         [
             pltpu.VMEM((count * 3, cols), F32),
-            pltpu.VMEM((padded, 2 * LANES), F32),
             pltpu.SemaphoreType.DMA((padded // CHUNK_OUT,)),
         ],
         (vm, vm, vm, hbm),
         hbm,
         "faces",
         {3: 0},
-    )(kept, tab, yrecv, col.reshape(count * 3, rows, cols))
+    )(kept, wide, yrecv, col.reshape(count * 3, rows, cols))
     return out.reshape(state.shape)
 
 

time: 20.6 us -> 20.1 us (0.976)
  Pallas kernels: 10.2 us -> 9.85 us
  waiting for transfers between devices: 1.29 us -> 0.97 us
    pallas_call x0 -> x1, Pallas kernels: none -> 0.54 us  [shards(): call(functools.partial(edge_kernel, count, rows), shape((SUB, padded // 2...]
    pallas_call x1, Pallas kernels: 3.73 us -> 3.31 us  [shards(): call(functools.partial(pre_kernel, count, rows), (shape((count, cols), F3...]
    pallas_call x1, Pallas kernels: 2.48 us -> 2.12 us  [shards(): call(functools.partial(transport_kernel, count, rows, cols, single), shap...]
    ppermute x3, waiting for transfers between devices: 1.18 us -> 0.91 us  [sum_over(): lax.ppermute(value, axis, [(i, i ^ step) for i in range(devices)])]
  transfers between devices with their start and end apart: 5 -> 5, of which waited for: 3 -> 3; matrix products, arithmetic and copies ran while one was open for 0% -> 0% of each run, Pallas kernels for 25% -> 27%
where the time goes in v4:
time: 20.1 us; the launch traced here: 19.9 us
  Pallas kernels  9.85 us (49%)
  starting transfers between devices  8.96 us (45%)
  waiting for transfers between devices  0.97 us (5%)
    ppermute x3, starting transfers between devices, sum_over(): lax.ppermute(value, axis, [(i, i ^ step) for i in range(devices)])  4.82 us
    pallas_call x1, Pallas kernels, shards(): call(functools.partial(pre_kernel, count, rows), (shape((count, cols), F3...  3.31 us
    pallas_call x1, Pallas kernels, shards(): call(functools.partial(collide_kernel, count, rows), (shape((total_rows,...  2.65 us
    ppermute x1, starting transfers between devices, shards(): yrecv = lax.ppermute(ysend, 'gy', [(0, 1), (1, 0)])  2.56 us
    pallas_call x1, Pallas kernels, shards(): call(functools.partial(transport_kernel, count, rows, cols, single), shap...  2.12 us
    ppermute x1, starting transfers between devices, exchange(): lax.ppermute(value, axis, [(i, (i + by) % devices) for i in range(devices)])  1.57 us
    pallas_call x1, Pallas kernels, shards(): call(functools.partial(face_kernel, count, rows), shape((count * 3, rows,...  1.22 us
    ppermute x3, waiting for transfers between devices, sum_over(): lax.ppermute(value, axis, [(i, i ^ step) for i in range(devices)])  0.91 us
  transfers between devices with their start and end apart: 5, of which 3 were waited for; matrix products, arithmetic and copies ran while one was open for 0% of the time, Pallas kernels for 27%

profile of v4, /device:TPU:0, one launch (start us, length us, event | category | flops | bytes accessed | tf_op | source)
XLA Modules:
  0.0 19.9 jit_solution(5851369968872007304)
XLA Ops:
  0.0 3.3 %pack_and_moments.1 = (f32[1000,128]{1,0:T(8,128)S(1)}, f32[120,128]{1,0:T(8,128)S(1)}, bf16[1024,128]{1,0:T(8,128)(2,1)S(1)}, f32[6144,128]{1,0:T(8,128)S(1)}, f32[4096,128]{1,0:T(8,128)S(1)}) custom-call(s32[2,1000]{1,0:T(2,128)} %bitcast.8, f32[6000,128]{1,0:T(8,128)} %bitcast.6, f32[6000,128]{1,0:T(8,128)} %bitcast.7), custom_call_target="tpu_custom_call" | custom-call | tf_op jit(solution)/shard_map/pack_and_moments/pallas_call | solution.py:514
  3.3 0.0 copy-start
  3.3 0.5 %collective-permute-start = (f32[120,128]{1,0:T(8,128)S(1)}, f32[120,128]{1,0:T(8,128)S(1)}, u32[]{:S(2)}, u32[]{:S(2)}) collective-permute-start(f32[120,128]{1,0:T(8,128)S(1)} %get-tuple-element.12), channel_id=1, source_target_pairs={{0,1},{1,0},{2,3},{3,2},{4,5},{5,4},{6,7},{7,6},{8,9},{9,8},{10,11... | collective-permute-start | bytes 184328 | tf_op jit(solution)/shard_map/ppermute | solution.py:497
  3.8 2.6 %collective-permute-start.4 = (f32[1000,128]{1,0:T(8,128)S(1)}, f32[1000,128]{1,0:T(8,128)S(1)}, u32[]{:S(2)}, u32[]{:S(2)}) collective-permute-start(f32[1000,128]{1,0:T(8,128)S(1)} %get-tuple-element.17), channel_id=1, source_target_pairs={{0,8},{8,0},{1,9},{9,1},{2,10},{10,2},{3,11},{11,3},{4,12},{12,4},... | collective-permute-start | bytes 1536008 | tf_op jit(solution)/shard_map/ppermute | solution.py:534
  6.4 0.0 collective-permute-done
  6.4 1.7 %collective-permute-start.1 = (f32[120,128]{1,0:T(8,128)S(1)}, f32[120,128]{1,0:T(8,128)S(1)}, u32[]{:S(2)}, u32[]{:S(2)}) collective-permute-start(f32[120,128]{1,0:T(8,128)S(1)} %add.9), channel_id=1, source_target_pairs={{0,2},{1,3},{2,0},{3,1},{4,6},{5,7},{6,4},{7,5},{8,10},{9,11},{10,... | collective-permute-start | bytes 184328 | tf_op jit(solution)/shard_map/ppermute | solution.py:497
  8.1 0.5 %edges.1 = f32[8,512]{1,0:T(8,128)S(1)} custom-call(f32[6144,128]{1,0:T(8,128)S(1)} %get-tuple-element.14.tan_v.refs_0_, f32[4096,128]{1,0:T(8,128)S(1)} %get-tuple-element.15.wide.refs_1_), custom_call_target="tpu_custom_call" | custom-call | tf_op jit(solution)/shard_map/edges/pallas_call | solution.py:535
  8.6 1.6 %collective-permute-start.3 = (f32[8,512]{1,0:T(8,128)S(1)}, f32[8,512]{1,0:T(8,128)S(1)}, u32[]{:S(2)}, u32[]{:S(2)}) collective-permute-start(f32[8,512]{1,0:T(8,128)S(1)} %edges.1), channel_id=1, source_target_pairs={{0,16},{16,0},{1,17},{17,1},{2,18},{18,2},{3,19},{19,3},{4,20},{20... | collective-permute-start | bytes 49160 | tf_op jit(solution)/shard_map/ppermute | solution.py:490
  10.2 0.5 %collective-permute-done.1 = f32[120,128]{1,0:T(8,128)S(1)} collective-permute-done((f32[120,128]{1,0:T(8,128)S(1)}, f32[120,128]{1,0:T(8,128)S(1)}, u32[]{:S(2)}, u32[]{:S(2)}) %collective-permute-start.1) | collective-permute-done | bytes 61472 | tf_op jit(solution)/shard_map/ppermute | solution.py:497
  10.7 2.7 %collective-permute-start.2 = (f32[120,128]{1,0:T(8,128)S(1)}, f32[120,128]{1,0:T(8,128)S(1)}, u32[]{:S(2)}, u32[]{:S(2)}) collective-permute-start(f32[120,128]{1,0:T(8,128)S(1)} %add.10), channel_id=1, source_target_pairs={{0,4},{1,5},{2,6},{3,7},{4,0},{5,1},{6,2},{7,3},{8,12},{9,13},{10,... | collective-permute-start | bytes 184328 | tf_op jit(solution)/shard_map/ppermute | solution.py:497
  13.4 0.0 collective-permute-done.3.refs_3_
  13.4 0.0 copy-done
  13.4 2.1 %transport.1.adv = f32[6000,128]{1,0:T(8,128)S(1)} custom-call(f32[6144,128]{1,0:T(8,128)S(1)} %get-tuple-element.14.tan_v.refs_0_, f32[4096,128]{1,0:T(8,128)S(1)} %get-tuple-element.15.wide.refs_1_, s32[2,128]{1,0:T(2,128)S(1)} %copy-done, f32[8,512]{1,0:T(8,128)S(1)} %collective-permute-done.3.refs_3_), custom_call_target="tpu_custom_call" | custom-call | flops 4499999744 | tf_op jit(solution)/shard_map/transport/pallas_call | solution.py:546
  15.5 0.4 %collective-permute-done.2 = f32[120,128]{1,0:T(8,128)S(1)} collective-permute-done((f32[120,128]{1,0:T(8,128)S(1)}, f32[120,128]{1,0:T(8,128)S(1)}, u32[]{:S(2)}, u32[]{:S(2)}) %collective-permute-start.2) | collective-permute-done | bytes 61472 | tf_op jit(solution)/shard_map/ppermute | solution.py:497
  15.9 2.7 %collide.1 = (f32[6000,128]{1,0:T(8,128)}, f32[3000,128]{1,0:T(8,128)S(1)}) custom-call(f32[120,128]{1,0:T(8,128)S(1)} %add.11.mom, bf16[1024,128]{1,0:T(8,128)(2,1)S(1)} %get-tuple-element.13.tab, f32[6000,128]{1,0:T(8,128)S(1)} %transport.1.adv), custom_call_target="tpu_custom_call" | custom-call | tf_op jit(solution)/shard_map/collide/pallas_call | solution.py:555
  18.6 0.1 collective-permute-done.4.yrecv
  18.7 1.2 %faces.1 = f32[3000,2,128]{2,1,0:T(2,128)} custom-call(f32[3000,128]{1,0:T(8,128)S(1)} %get-tuple-element.16.kept, f32[4096,128]{1,0:T(8,128)S(1)} %get-tuple-element.15.wide.refs_1_, f32[1000,128]{1,0:T(8,128)S(1)} %collective-permute-done.4.yrecv, f32[3000,2,128]{2,1,0:T(2,128)} %bitcast.5), custom_call_target="tpu_custom_call", output_to_operand_aliasing={{}: (3, {})} | custom-call | tf_op jit(solution)/shard_map/faces/pallas_call | solution.py:570
  (3 shorter events, 0.0 us)
Async XLA Ops:
  3.3 10.1 %copy-start = (s32[2,128]{1,0:T(2,128)S(1)}, s32[2,128]{1,0:T(2,128)}, u32[]{:S(2)}) copy-start(s32[2,128]{1,0:T(2,128)} %refs_2_.1) | copy-start | bytes 3076
  3.3 3.1 %collective-permute-start = (f32[120,128]{1,0:T(8,128)S(1)}, f32[120,128]{1,0:T(8,128)S(1)}, u32[]{:S(2)}, u32[]{:S(2)}) collective-permute-start(f32[120,128]{1,0:T(8,128)S(1)} %get-tuple-element.12), channel_id=1, source_target_pairs={{0,1},{1,0},{2,3},{3,2},{4,5},{5,4},{6,7},{7,6},{8,9},{9,8},{10,11... | collective-permute-start | bytes 184328 | tf_op jit(solution)/shard_map/ppermute | solution.py:497
  3.8 14.8 %collective-permute-start.4 = (f32[1000,128]{1,0:T(8,128)S(1)}, f32[1000,128]{1,0:T(8,128)S(1)}, u32[]{:S(2)}, u32[]{:S(2)}) collective-permute-start(f32[1000,128]{1,0:T(8,128)S(1)} %get-tuple-element.17), channel_id=1, source_target_pairs={{0,8},{8,0},{1,9},{9,1},{2,10},{10,2},{3,11},{11,3},{4,12},{12,4},... | collective-permute-start | bytes 1536008 | tf_op jit(solution)/shard_map/ppermute | solution.py:534
  6.4 4.3 %collective-permute-start.1 = (f32[120,128]{1,0:T(8,128)S(1)}, f32[120,128]{1,0:T(8,128)S(1)}, u32[]{:S(2)}, u32[]{:S(2)}) collective-permute-start(f32[120,128]{1,0:T(8,128)S(1)} %add.9), channel_id=1, source_target_pairs={{0,2},{1,3},{2,0},{3,1},{4,6},{5,7},{6,4},{7,5},{8,10},{9,11},{10,... | collective-permute-start | bytes 184328 | tf_op jit(solution)/shard_map/ppermute | solution.py:497
  8.6 4.7 %collective-permute-start.3 = (f32[8,512]{1,0:T(8,128)S(1)}, f32[8,512]{1,0:T(8,128)S(1)}, u32[]{:S(2)}, u32[]{:S(2)}) collective-permute-start(f32[8,512]{1,0:T(8,128)S(1)} %edges.1), channel_id=1, source_target_pairs={{0,16},{16,0},{1,17},{17,1},{2,18},{18,2},{3,19},{19,3},{4,20},{20... | collective-permute-start | bytes 49160 | tf_op jit(solution)/shard_map/ppermute | solution.py:490
  10.7 5.2 %collective-permute-start.2 = (f32[120,128]{1,0:T(8,128)S(1)}, f32[120,128]{1,0:T(8,128)S(1)}, u32[]{:S(2)}, u32[]{:S(2)}) collective-permute-start(f32[120,128]{1,0:T(8,128)S(1)} %add.10), channel_id=1, source_target_pairs={{0,4},{1,5},{2,6},{3,7},{4,0},{5,1},{6,2},{7,3},{8,12},{9,13},{10,... | collective-permute-start | bytes 184328 | tf_op jit(solution)/shard_map/ppermute | solution.py:497

commit v5 on v4

--- a/solution.py
+++ b/solution.py
@@ -20,12 +20,11 @@
 UNIT = 0.5 * SPACING
 FEATS = 16
 SUB = 8
-IN_FLIGHT = 64
 WORK = 4500 * 10**6
 LANES = 128
-CHUNK = 256
+CHUNK = 512
 CHUNK_OUT = 128
-U_PACK, U_EDGE, U_TRANS, U_COLL, U_FACE = 32, 31, 16, 16, 16
+U_PACK, U_EDGE, U_TRANS, U_COLL, U_FACE = 64, 31, 16, 16, 16
 F32 = jnp.float32
 BF16 = jnp.bfloat16
 VMEM_LIMIT = 16 * 1024 * 1024
@@ -125,8 +124,8 @@
             copies.append(pltpu.make_async_copy(src.at[part], dst.at[part], sems.at[a * len(starts) + j]))
     signs = pltpu.make_async_copy(orient_hbm, orient_ref, sems.at[2 * len(starts)])
     signs.start()
-    for copy in copies[:IN_FLIGHT]:
-        copy.start()
+    for i, copy in enumerate(copies):
+        copy.start(priority=0 if i < len(starts) else 1)
     tail = (padded - count) * comps
     for buf in (tan_v, st_v):
         if tail:
@@ -148,8 +147,6 @@
     for a, buf in enumerate((tan_v, st_v)):
         for j, start in enumerate(starts):
             copies[a * len(starts) + j].wait()
-            for copy in copies[a * len(starts) + j + IN_FLIGHT :][:1]:
-                copy.start()
 
             def pack(local):
                 first = start + local

time: 20.1 us -> 20 us (level)
  no operation moved by 1% of the time
where the time goes in v5:
time: 20 us; the launch traced here: 19.8 us
  Pallas kernels  9.73 us (49%)
  starting transfers between devices  8.96 us (45%)
  waiting for transfers between devices  0.98 us (5%)
    ppermute x3, starting transfers between devices, sum_over(): lax.ppermute(value, axis, [(i, i ^ step) for i in range(devices)])  4.81 us
    pallas_call x1, Pallas kernels, shards(): call(functools.partial(pre_kernel, count, rows), (shape((count, cols), F3...  3.19 us
    pallas_call x1, Pallas kernels, shards(): call(functools.partial(collide_kernel, count, rows), (shape((total_rows,...  2.65 us
    ppermute x1, starting transfers between devices, shards(): yrecv = lax.ppermute(ysend, 'gy', [(0, 1), (1, 0)])  2.56 us
    pallas_call x1, Pallas kernels, shards(): call(functools.partial(transport_kernel, count, rows, cols, single), shap...  2.12 us
    ppermute x1, starting transfers between devices, exchange(): lax.ppermute(value, axis, [(i, (i + by) % devices) for i in range(devices)])  1.59 us
    pallas_call x1, Pallas kernels, shards(): call(functools.partial(face_kernel, count, rows), shape((count * 3, rows,...  1.22 us
    ppermute x3, waiting for transfers between devices, sum_over(): lax.ppermute(value, axis, [(i, i ^ step) for i in range(devices)])  0.91 us
  transfers between devices with their start and end apart: 5, of which 3 were waited for; matrix products, arithmetic and copies ran while one was open for 0% of the time, Pallas kernels for 27%

profile of v5, /device:TPU:0, one launch (start us, length us, event | category | flops | bytes accessed | tf_op | source)
XLA Modules:
  0.0 19.8 jit_solution(11322271715065643769)
XLA Ops:
  0.0 3.2 %pack_and_moments.1 = (f32[1000,128]{1,0:T(8,128)S(1)}, f32[120,128]{1,0:T(8,128)S(1)}, bf16[1024,128]{1,0:T(8,128)(2,1)S(1)}, f32[6144,128]{1,0:T(8,128)S(1)}, f32[4096,128]{1,0:T(8,128)S(1)}) custom-call(s32[2,1000]{1,0:T(2,128)} %bitcast.8, f32[6000,128]{1,0:T(8,128)} %bitcast.6, f32[6000,128]{1,0:T(8,128)} %bitcast.7), custom_call_target="tpu_custom_call" | custom-call | tf_op jit(solution)/shard_map/pack_and_moments/pallas_call | solution.py:511
  3.2 0.0 copy-start
  3.2 0.5 %collective-permute-start = (f32[120,128]{1,0:T(8,128)S(1)}, f32[120,128]{1,0:T(8,128)S(1)}, u32[]{:S(2)}, u32[]{:S(2)}) collective-permute-start(f32[120,128]{1,0:T(8,128)S(1)} %get-tuple-element.12), channel_id=1, source_target_pairs={{0,1},{1,0},{2,3},{3,2},{4,5},{5,4},{6,7},{7,6},{8,9},{9,8},{10,11... | collective-permute-start | bytes 184328 | tf_op jit(solution)/shard_map/ppermute | solution.py:494
  3.7 2.6 %collective-permute-start.4 = (f32[1000,128]{1,0:T(8,128)S(1)}, f32[1000,128]{1,0:T(8,128)S(1)}, u32[]{:S(2)}, u32[]{:S(2)}) collective-permute-start(f32[1000,128]{1,0:T(8,128)S(1)} %get-tuple-element.17), channel_id=1, source_target_pairs={{0,8},{8,0},{1,9},{9,1},{2,10},{10,2},{3,11},{11,3},{4,12},{12,4},... | collective-permute-start | bytes 1536008 | tf_op jit(solution)/shard_map/ppermute | solution.py:531
  6.3 0.0 collective-permute-done
  6.3 1.6 %collective-permute-start.1 = (f32[120,128]{1,0:T(8,128)S(1)}, f32[120,128]{1,0:T(8,128)S(1)}, u32[]{:S(2)}, u32[]{:S(2)}) collective-permute-start(f32[120,128]{1,0:T(8,128)S(1)} %add.9), channel_id=1, source_target_pairs={{0,2},{1,3},{2,0},{3,1},{4,6},{5,7},{6,4},{7,5},{8,10},{9,11},{10,... | collective-permute-start | bytes 184328 | tf_op jit(solution)/shard_map/ppermute | solution.py:494
  7.9 0.5 %edges.1 = f32[8,512]{1,0:T(8,128)S(1)} custom-call(f32[6144,128]{1,0:T(8,128)S(1)} %get-tuple-element.14.tan_v.refs_0_, f32[4096,128]{1,0:T(8,128)S(1)} %get-tuple-element.15.wide.refs_1_), custom_call_target="tpu_custom_call" | custom-call | tf_op jit(solution)/shard_map/edges/pallas_call | solution.py:532
  8.5 1.6 %collective-permute-start.3 = (f32[8,512]{1,0:T(8,128)S(1)}, f32[8,512]{1,0:T(8,128)S(1)}, u32[]{:S(2)}, u32[]{:S(2)}) collective-permute-start(f32[8,512]{1,0:T(8,128)S(1)} %edges.1), channel_id=1, source_target_pairs={{0,16},{16,0},{1,17},{17,1},{2,18},{18,2},{3,19},{19,3},{4,20},{20... | collective-permute-start | bytes 49160 | tf_op jit(solution)/shard_map/ppermute | solution.py:487
  10.1 0.5 %collective-permute-done.1 = f32[120,128]{1,0:T(8,128)S(1)} collective-permute-done((f32[120,128]{1,0:T(8,128)S(1)}, f32[120,128]{1,0:T(8,128)S(1)}, u32[]{:S(2)}, u32[]{:S(2)}) %collective-permute-start.1) | collective-permute-done | bytes 61472 | tf_op jit(solution)/shard_map/ppermute | solution.py:494
  10.6 2.7 %collective-permute-start.2 = (f32[120,128]{1,0:T(8,128)S(1)}, f32[120,128]{1,0:T(8,128)S(1)}, u32[]{:S(2)}, u32[]{:S(2)}) collective-permute-start(f32[120,128]{1,0:T(8,128)S(1)} %add.10), channel_id=1, source_target_pairs={{0,4},{1,5},{2,6},{3,7},{4,0},{5,1},{6,2},{7,3},{8,12},{9,13},{10,... | collective-permute-start | bytes 184328 | tf_op jit(solution)/shard_map/ppermute | solution.py:494
  13.3 0.0 collective-permute-done.3.refs_3_
  13.3 0.0 copy-done
  13.3 2.1 %transport.1.adv = f32[6000,128]{1,0:T(8,128)S(1)} custom-call(f32[6144,128]{1,0:T(8,128)S(1)} %get-tuple-element.14.tan_v.refs_0_, f32[4096,128]{1,0:T(8,128)S(1)} %get-tuple-element.15.wide.refs_1_, s32[2,128]{1,0:T(2,128)S(1)} %copy-done, f32[8,512]{1,0:T(8,128)S(1)} %collective-permute-done.3.refs_3_), custom_call_target="tpu_custom_call" | custom-call | flops 4499999744 | tf_op jit(solution)/shard_map/transport/pallas_call | solution.py:543
  15.4 0.4 %collective-permute-done.2 = f32[120,128]{1,0:T(8,128)S(1)} collective-permute-done((f32[120,128]{1,0:T(8,128)S(1)}, f32[120,128]{1,0:T(8,128)S(1)}, u32[]{:S(2)}, u32[]{:S(2)}) %collective-permute-start.2) | collective-permute-done | bytes 61472 | tf_op jit(solution)/shard_map/ppermute | solution.py:494
  15.8 2.7 %collide.1 = (f32[6000,128]{1,0:T(8,128)}, f32[3000,128]{1,0:T(8,128)S(1)}) custom-call(f32[120,128]{1,0:T(8,128)S(1)} %add.11.mom, bf16[1024,128]{1,0:T(8,128)(2,1)S(1)} %get-tuple-element.13.tab, f32[6000,128]{1,0:T(8,128)S(1)} %transport.1.adv), custom_call_target="tpu_custom_call" | custom-call | tf_op jit(solution)/shard_map/collide/pallas_call | solution.py:552
  18.5 0.1 collective-permute-done.4.yrecv
  18.5 1.2 %faces.1 = f32[3000,2,128]{2,1,0:T(2,128)} custom-call(f32[3000,128]{1,0:T(8,128)S(1)} %get-tuple-element.16.kept, f32[4096,128]{1,0:T(8,128)S(1)} %get-tuple-element.15.wide.refs_1_, f32[1000,128]{1,0:T(8,128)S(1)} %collective-permute-done.4.yrecv, f32[3000,2,128]{2,1,0:T(2,128)} %bitcast.5), custom_call_target="tpu_custom_call", output_to_operand_aliasing={{}: (3, {})} | custom-call | tf_op jit(solution)/shard_map/faces/pallas_call | solution.py:567
  (3 shorter events, 0.0 us)
Async XLA Ops:
  3.2 10.1 %copy-start = (s32[2,128]{1,0:T(2,128)S(1)}, s32[2,128]{1,0:T(2,128)}, u32[]{:S(2)}) copy-start(s32[2,128]{1,0:T(2,128)} %refs_2_.1) | copy-start | bytes 3076
  3.2 3.1 %collective-permute-start = (f32[120,128]{1,0:T(8,128)S(1)}, f32[120,128]{1,0:T(8,128)S(1)}, u32[]{:S(2)}, u32[]{:S(2)}) collective-permute-start(f32[120,128]{1,0:T(8,128)S(1)} %get-tuple-element.12), channel_id=1, source_target_pairs={{0,1},{1,0},{2,3},{3,2},{4,5},{5,4},{6,7},{7,6},{8,9},{9,8},{10,11... | collective-permute-start | bytes 184328 | tf_op jit(solution)/shard_map/ppermute | solution.py:494
  3.7 14.8 %collective-permute-start.4 = (f32[1000,128]{1,0:T(8,128)S(1)}, f32[1000,128]{1,0:T(8,128)S(1)}, u32[]{:S(2)}, u32[]{:S(2)}) collective-permute-start(f32[1000,128]{1,0:T(8,128)S(1)} %get-tuple-element.17), channel_id=1, source_target_pairs={{0,8},{8,0},{1,9},{9,1},{2,10},{10,2},{3,11},{11,3},{4,12},{12,4},... | collective-permute-start | bytes 1536008 | tf_op jit(solution)/shard_map/ppermute | solution.py:531
  6.3 4.3 %collective-permute-start.1 = (f32[120,128]{1,0:T(8,128)S(1)}, f32[120,128]{1,0:T(8,128)S(1)}, u32[]{:S(2)}, u32[]{:S(2)}) collective-permute-start(f32[120,128]{1,0:T(8,128)S(1)} %add.9), channel_id=1, source_target_pairs={{0,2},{1,3},{2,0},{3,1},{4,6},{5,7},{6,4},{7,5},{8,10},{9,11},{10,... | collective-permute-start | bytes 184328 | tf_op jit(solution)/shard_map/ppermute | solution.py:494
  8.5 4.7 %collective-permute-start.3 = (f32[8,512]{1,0:T(8,128)S(1)}, f32[8,512]{1,0:T(8,128)S(1)}, u32[]{:S(2)}, u32[]{:S(2)}) collective-permute-start(f32[8,512]{1,0:T(8,128)S(1)} %edges.1), channel_id=1, source_target_pairs={{0,16},{16,0},{1,17},{17,1},{2,18},{18,2},{3,19},{19,3},{4,20},{20... | collective-permute-start | bytes 49160 | tf_op jit(solution)/shard_map/ppermute | solution.py:487
  10.6 5.2 %collective-permute-start.2 = (f32[120,128]{1,0:T(8,128)S(1)}, f32[120,128]{1,0:T(8,128)S(1)}, u32[]{:S(2)}, u32[]{:S(2)}) collective-permute-start(f32[120,128]{1,0:T(8,128)S(1)} %add.10), channel_id=1, source_target_pairs={{0,4},{1,5},{2,6},{3,7},{4,0},{5,1},{6,2},{7,3},{8,12},{9,13},{10,... | collective-permute-start | bytes 184328 | tf_op jit(solution)/shard_map/ppermute | solution.py:494

commit v6 on v5

--- a/solution.py
+++ b/solution.py
@@ -463,7 +463,7 @@
         for_blocks(size, block, U_FACE)
         part = pl.ds(start * 3, size * 3)
         copies.append(pltpu.make_async_copy(face_v.at[part], out.at[part, face], sems.at[j]))
-        copies[-1].start()
+        copies[-1].start(priority=j % 2)
     for copy in copies:
         copy.wait()
 

time: 20 us -> 20 us (level)
  no operation moved by 1% of the time
where the time goes in v6:
time: 20 us; the launch traced here: 19.8 us
  Pallas kernels  9.73 us (49%)
  starting transfers between devices  8.96 us (45%)
  waiting for transfers between devices  0.98 us (5%)
    ppermute x3, starting transfers between devices, sum_over(): lax.ppermute(value, axis, [(i, i ^ step) for i in range(devices)])  4.81 us
    pallas_call x1, Pallas kernels, shards(): call(functools.partial(pre_kernel, count, rows), (shape((count, cols), F3...  3.19 us
    pallas_call x1, Pallas kernels, shards(): call(functools.partial(collide_kernel, count, rows), (shape((total_rows,...  2.65 us
    ppermute x1, starting transfers between devices, shards(): yrecv = lax.ppermute(ysend, 'gy', [(0, 1), (1, 0)])  2.56 us
    pallas_call x1, Pallas kernels, shards(): call(functools.partial(transport_kernel, count, rows, cols, single), shap...  2.12 us
    ppermute x1, starting transfers between devices, exchange(): lax.ppermute(value, axis, [(i, (i + by) % devices) for i in range(devices)])  1.59 us
    pallas_call x1, Pallas kernels, shards(): call(functools.partial(face_kernel, count, rows), shape((count * 3, rows,...  1.23 us
    ppermute x3, waiting for transfers between devices, sum_over(): lax.ppermute(value, axis, [(i, i ^ step) for i in range(devices)])  0.91 us
  transfers between devices with their start and end apart: 5, of which 3 were waited for; matrix products, arithmetic and copies ran while one was open for 0% of the time, Pallas kernels for 27%

profile of v6, /device:TPU:0, one launch (start us, length us, event | category | flops | bytes accessed | tf_op | source)
XLA Modules:
  0.0 19.8 jit_solution(7286135044348240275)
XLA Ops:
  0.0 3.2 %pack_and_moments.1 = (f32[1000,128]{1,0:T(8,128)S(1)}, f32[120,128]{1,0:T(8,128)S(1)}, bf16[1024,128]{1,0:T(8,128)(2,1)S(1)}, f32[6144,128]{1,0:T(8,128)S(1)}, f32[4096,128]{1,0:T(8,128)S(1)}) custom-call(s32[2,1000]{1,0:T(2,128)} %bitcast.8, f32[6000,128]{1,0:T(8,128)} %bitcast.6, f32[6000,128]{1,0:T(8,128)} %bitcast.7), custom_call_target="tpu_custom_call" | custom-call | tf_op jit(solution)/shard_map/pack_and_moments/pallas_call | solution.py:511
  3.2 0.0 copy-start
  3.2 0.5 %collective-permute-start = (f32[120,128]{1,0:T(8,128)S(1)}, f32[120,128]{1,0:T(8,128)S(1)}, u32[]{:S(2)}, u32[]{:S(2)}) collective-permute-start(f32[120,128]{1,0:T(8,128)S(1)} %get-tuple-element.12), channel_id=1, source_target_pairs={{0,1},{1,0},{2,3},{3,2},{4,5},{5,4},{6,7},{7,6},{8,9},{9,8},{10,11... | collective-permute-start | bytes 184328 | tf_op jit(solution)/shard_map/ppermute | solution.py:494
  3.7 2.6 %collective-permute-start.4 = (f32[1000,128]{1,0:T(8,128)S(1)}, f32[1000,128]{1,0:T(8,128)S(1)}, u32[]{:S(2)}, u32[]{:S(2)}) collective-permute-start(f32[1000,128]{1,0:T(8,128)S(1)} %get-tuple-element.17), channel_id=1, source_target_pairs={{0,8},{8,0},{1,9},{9,1},{2,10},{10,2},{3,11},{11,3},{4,12},{12,4},... | collective-permute-start | bytes 1536008 | tf_op jit(solution)/shard_map/ppermute | solution.py:531
  6.3 0.0 collective-permute-done
  6.3 1.6 %collective-permute-start.1 = (f32[120,128]{1,0:T(8,128)S(1)}, f32[120,128]{1,0:T(8,128)S(1)}, u32[]{:S(2)}, u32[]{:S(2)}) collective-permute-start(f32[120,128]{1,0:T(8,128)S(1)} %add.9), channel_id=1, source_target_pairs={{0,2},{1,3},{2,0},{3,1},{4,6},{5,7},{6,4},{7,5},{8,10},{9,11},{10,... | collective-permute-start | bytes 184328 | tf_op jit(solution)/shard_map/ppermute | solution.py:494
  7.9 0.5 %edges.1 = f32[8,512]{1,0:T(8,128)S(1)} custom-call(f32[6144,128]{1,0:T(8,128)S(1)} %get-tuple-element.14.tan_v.refs_0_, f32[4096,128]{1,0:T(8,128)S(1)} %get-tuple-element.15.wide.refs_1_), custom_call_target="tpu_custom_call" | custom-call | tf_op jit(solution)/shard_map/edges/pallas_call | solution.py:532
  8.5 1.6 %collective-permute-start.3 = (f32[8,512]{1,0:T(8,128)S(1)}, f32[8,512]{1,0:T(8,128)S(1)}, u32[]{:S(2)}, u32[]{:S(2)}) collective-permute-start(f32[8,512]{1,0:T(8,128)S(1)} %edges.1), channel_id=1, source_target_pairs={{0,16},{16,0},{1,17},{17,1},{2,18},{18,2},{3,19},{19,3},{4,20},{20... | collective-permute-start | bytes 49160 | tf_op jit(solution)/shard_map/ppermute | solution.py:487
  10.1 0.5 %collective-permute-done.1 = f32[120,128]{1,0:T(8,128)S(1)} collective-permute-done((f32[120,128]{1,0:T(8,128)S(1)}, f32[120,128]{1,0:T(8,128)S(1)}, u32[]{:S(2)}, u32[]{:S(2)}) %collective-permute-start.1) | collective-permute-done | bytes 61472 | tf_op jit(solution)/shard_map/ppermute | solution.py:494
  10.6 2.7 %collective-permute-start.2 = (f32[120,128]{1,0:T(8,128)S(1)}, f32[120,128]{1,0:T(8,128)S(1)}, u32[]{:S(2)}, u32[]{:S(2)}) collective-permute-start(f32[120,128]{1,0:T(8,128)S(1)} %add.10), channel_id=1, source_target_pairs={{0,4},{1,5},{2,6},{3,7},{4,0},{5,1},{6,2},{7,3},{8,12},{9,13},{10,... | collective-permute-start | bytes 184328 | tf_op jit(solution)/shard_map/ppermute | solution.py:494
  13.3 0.0 collective-permute-done.3.refs_3_
  13.3 0.0 copy-done
  13.3 2.1 %transport.1.adv = f32[6000,128]{1,0:T(8,128)S(1)} custom-call(f32[6144,128]{1,0:T(8,128)S(1)} %get-tuple-element.14.tan_v.refs_0_, f32[4096,128]{1,0:T(8,128)S(1)} %get-tuple-element.15.wide.refs_1_, s32[2,128]{1,0:T(2,128)S(1)} %copy-done, f32[8,512]{1,0:T(8,128)S(1)} %collective-permute-done.3.refs_3_), custom_call_target="tpu_custom_call" | custom-call | flops 4499999744 | tf_op jit(solution)/shard_map/transport/pallas_call | solution.py:543
  15.4 0.4 %collective-permute-done.2 = f32[120,128]{1,0:T(8,128)S(1)} collective-permute-done((f32[120,128]{1,0:T(8,128)S(1)}, f32[120,128]{1,0:T(8,128)S(1)}, u32[]{:S(2)}, u32[]{:S(2)}) %collective-permute-start.2) | collective-permute-done | bytes 61472 | tf_op jit(solution)/shard_map/ppermute | solution.py:494
  15.8 2.7 %collide.1 = (f32[6000,128]{1,0:T(8,128)}, f32[3000,128]{1,0:T(8,128)S(1)}) custom-call(f32[120,128]{1,0:T(8,128)S(1)} %add.11.mom, bf16[1024,128]{1,0:T(8,128)(2,1)S(1)} %get-tuple-element.13.tab, f32[6000,128]{1,0:T(8,128)S(1)} %transport.1.adv), custom_call_target="tpu_custom_call" | custom-call | tf_op jit(solution)/shard_map/collide/pallas_call | solution.py:552
  18.5 0.1 collective-permute-done.4.yrecv
  18.5 1.2 %faces.1 = f32[3000,2,128]{2,1,0:T(2,128)} custom-call(f32[3000,128]{1,0:T(8,128)S(1)} %get-tuple-element.16.kept, f32[4096,128]{1,0:T(8,128)S(1)} %get-tuple-element.15.wide.refs_1_, f32[1000,128]{1,0:T(8,128)S(1)} %collective-permute-done.4.yrecv, f32[3000,2,128]{2,1,0:T(2,128)} %bitcast.5), custom_call_target="tpu_custom_call", output_to_operand_aliasing={{}: (3, {})} | custom-call | tf_op jit(solution)/shard_map/faces/pallas_call | solution.py:567
  (3 shorter events, 0.0 us)
Async XLA Ops:
  3.2 10.1 %copy-start = (s32[2,128]{1,0:T(2,128)S(1)}, s32[2,128]{1,0:T(2,128)}, u32[]{:S(2)}) copy-start(s32[2,128]{1,0:T(2,128)} %refs_2_.1) | copy-start | bytes 3076
  3.2 3.1 %collective-permute-start = (f32[120,128]{1,0:T(8,128)S(1)}, f32[120,128]{1,0:T(8,128)S(1)}, u32[]{:S(2)}, u32[]{:S(2)}) collective-permute-start(f32[120,128]{1,0:T(8,128)S(1)} %get-tuple-element.12), channel_id=1, source_target_pairs={{0,1},{1,0},{2,3},{3,2},{4,5},{5,4},{6,7},{7,6},{8,9},{9,8},{10,11... | collective-permute-start | bytes 184328 | tf_op jit(solution)/shard_map/ppermute | solution.py:494
  3.7 14.8 %collective-permute-start.4 = (f32[1000,128]{1,0:T(8,128)S(1)}, f32[1000,128]{1,0:T(8,128)S(1)}, u32[]{:S(2)}, u32[]{:S(2)}) collective-permute-start(f32[1000,128]{1,0:T(8,128)S(1)} %get-tuple-element.17), channel_id=1, source_target_pairs={{0,8},{8,0},{1,9},{9,1},{2,10},{10,2},{3,11},{11,3},{4,12},{12,4},... | collective-permute-start | bytes 1536008 | tf_op jit(solution)/shard_map/ppermute | solution.py:531
  6.3 4.3 %collective-permute-start.1 = (f32[120,128]{1,0:T(8,128)S(1)}, f32[120,128]{1,0:T(8,128)S(1)}, u32[]{:S(2)}, u32[]{:S(2)}) collective-permute-start(f32[120,128]{1,0:T(8,128)S(1)} %add.9), channel_id=1, source_target_pairs={{0,2},{1,3},{2,0},{3,1},{4,6},{5,7},{6,4},{7,5},{8,10},{9,11},{10,... | collective-permute-start | bytes 184328 | tf_op jit(solution)/shard_map/ppermute | solution.py:494
  8.5 4.7 %collective-permute-start.3 = (f32[8,512]{1,0:T(8,128)S(1)}, f32[8,512]{1,0:T(8,128)S(1)}, u32[]{:S(2)}, u32[]{:S(2)}) collective-permute-start(f32[8,512]{1,0:T(8,128)S(1)} %edges.1), channel_id=1, source_target_pairs={{0,16},{16,0},{1,17},{17,1},{2,18},{18,2},{3,19},{19,3},{4,20},{20... | collective-permute-start | bytes 49160 | tf_op jit(solution)/shard_map/ppermute | solution.py:487
  10.6 5.2 %collective-permute-start.2 = (f32[120,128]{1,0:T(8,128)S(1)}, f32[120,128]{1,0:T(8,128)S(1)}, u32[]{:S(2)}, u32[]{:S(2)}) collective-permute-start(f32[120,128]{1,0:T(8,128)S(1)} %add.10), channel_id=1, source_target_pairs={{0,4},{1,5},{2,6},{3,7},{4,0},{5,1},{6,2},{7,3},{8,12},{9,13},{10,... | collective-permute-start | bytes 184328 | tf_op jit(solution)/shard_map/ppermute | solution.py:494
